TPU v7x, 256 devices: a whole 4x4x8 slice. The times are simulated.
256 devices in a mesh: outer: 8 (over z_hi, core), inner: 32 (over y, x, z_lo).
Axes of the slice: x: 4, y: 4, z: 8 (z_hi: 4, z_lo: 2; z = z_hi * 2 + z_lo), core: 2. Of those that a mesh axis runs over, the one named last changes fastest.
Arguments:
- object_field: float32 [2, 2048, 8192], P(None, ('outer', 'inner')), may hold values from -6 to 6
- probe: float32 [2, 2048, 8192], P(None, ('outer', 'inner')), may hold values from -8 to 8
- intensity: float32 [2048, 8192], P(('outer', 'inner')), may hold values from 0.01 to 9
- row_offset: int32 [1], replicated, may hold values from 1 to 7
- col_offset: int32 [1], replicated, may hold values from 0 to 8191
Outputs:
- object_step: float32 [2, 2048, 8192], P(None, ('outer', 'inner'))
All inputs are finite; a program needn't handle non-finite values.
Results may differ from a plain program's by a relative error of at most 0.00013.
Values sent between devices are 32-bit elements; how exact they have to be, the bound alone decides.
A program may use at most 128 MiB of HBM per device.

v0:
```python
import math

import jax
import jax.numpy as jnp
import numpy as np
from jax import lax
from jax.experimental import pallas as pl
from jax.experimental.pallas import tpu as pltpu
from jax.sharding import PartitionSpec as P

FLOOR_LEVEL = 0.1
MESH = pl.DeviceIdType.MESH
CHIPS = 128
F32 = jnp.float32
BF16 = jnp.bfloat16


def split_table(table):
    table = np.asarray(table, np.float64).astype(np.float32)
    high = table.astype(jnp.bfloat16)
    low = (table - high.astype(np.float32)).astype(jnp.bfloat16)
    return np.stack([high, low])


def turn(numerator, modulus):
    angle = -2.0 * np.pi * (np.asarray(numerator) % modulus) / modulus
    return np.exp(1j * angle)


def expanded(table):
    return np.block([[table.real, table.imag], [-table.imag, table.real]])


def make_tables():
    tables = {}
    col = np.arange(8192, dtype=np.int64) - 4096
    col_phase = np.pi / 8192 * (col * col % 16384)
    tables["col_chirp"] = np.stack([np.cos(col_phase), np.sin(col_phase)]).reshape(2, 1, 8192).astype(np.float32)
    row = np.arange(2048, dtype=np.int64) - 1024
    row_phase = (np.pi / 2048 * (row * row % 4096)).reshape(256, 8).T
    tables["row_chirp"] = np.stack([np.cos(row_phase), np.sin(row_phase)]).astype(np.float32)
    order = np.concatenate([2 * np.arange(64), 2 * np.arange(64) + 1])
    first = turn(np.arange(128)[:, None] * order[None, :], 128)
    tables["first"] = split_table(np.concatenate([first.real, first.imag], axis=1))
    back = np.conj(first).T
    tables["first_back"] = split_table(np.concatenate([back.real, back.imag], axis=1))
    chip_turn = turn(np.arange(64)[:, None] * np.arange(128)[None, :], 8192)
    tables["chip_turn"] = np.stack([chip_turn.real, chip_turn.imag]).astype(np.float32)
    base = []
    for core in range(2):
        blocks = []
        for zh in range(4):
            halves = []
            for half in range(2):
                q = 32 * (core if half == 0 else 1 - core) + np.arange(32)
                klow = np.arange(4)
                m = np.arange(64)
                power = (
                    m[:, None, None] * q[None, None, :] * 8
                    + zh * klow[None, :, None] * 128
                    + core * klow[None, :, None] * 64
                )
                halves.append(expanded(turn(power, 512).reshape(64, 128)))
            blocks.append(np.concatenate(halves, axis=1))
        base.append(np.concatenate(blocks, axis=0))
    tables["base"] = np.stack(base).astype(np.float32)
    index = np.arange(256)
    zl, y, x, l = index // 128, index // 32 % 4, index // 8 % 4, index % 8
    n = 64 * y + 16 * x + 8 * zl + l
    last = turn(n[:, None] * n[None, :], 256)
    tables["last"] = split_table(np.block([[last.real, -last.imag], [last.imag, last.real]]))
    tables["last_back"] = split_table(np.block([[last.real, last.imag], [-last.imag, last.real]]))
    klow = np.arange(128) // 32
    twiddle = np.stack([turn(n[:, None] * (klow[None, :] + 4 * k2), 2048) for k2 in range(2)]) / 4096.0
    tables["twiddle"] = np.stack([twiddle.real, twiddle.imag], axis=1).astype(np.float32)
    return tables


TABLES = (
    "col_chirp",
    "row_chirp",
    "first",
    "first_back",
    "chip_turn",
    "base",
    "last",
    "last_back",
    "twiddle",
)


def split(value):
    high = value.astype(BF16)
    low = (value - high.astype(F32)).astype(BF16)
    return high, low


def dot(left, right):
    return jnp.dot(left, right, preferred_element_type=F32)


def dot_t(left, right):
    return lax.dot_general(left, right, (((1,), (1,)), ((), ())), preferred_element_type=F32)


def three(op, left, right):
    return op(left[0], right[0]) + (op(left[0], right[1]) + op(left[1], right[0]))


def device_of(chip, core):
    z = chip // 16
    return (z // 2) * 2 + core, (chip // 4 % 4) * 8 + (chip % 4) * 2 + z % 2


def flip(chip, offset):
    return chip ^ offset


def tile(ref, index):
    return ref.at[pl.ds(pl.multiple_of(index * 8, 8), 8)]


def kernel(
    row_off,
    col_off,
    obj_hbm,
    probe_hbm,
    int_hbm,
    col_chirp_hbm,
    row_chirp_hbm,
    first_hbm,
    first_back_hbm,
    chip_turn_hbm,
    base_hbm,
    last_hbm,
    last_back_hbm,
    twiddle_hbm,
    out_ref,
    peak_ref,
    obj,
    probe,
    inten,
    col_chirp,
    row_chirp,
    first,
    first_back,
    chip_turn,
    base,
    last,
    last_back,
    twiddle,
    rolled,
    arrived,
    wave,
    turned,
    field_out,
    field_in,
    mixed,
    mixed_out,
    factor,
    spread,
    shades_out,
    shades_in,
    back_out,
    back_in,
    part_out,
    part_in,
    peak_own,
    peak_z,
    peak_y,
    peak_x,
    peak_c,
    load_sem,
    shift_sem,
    int_sem,
    z_sem,
    y_sem,
    x_sem,
    c_sem,
    shade_sem,
    pass_sem,
    field_sem,
    mix_sem,
    part_sem,
    back_sem,
    local_sem,
):
    outer, inner = lax.axis_index("outer"), lax.axis_index("inner")
    zh, core = outer // 2, outer % 2
    other = 1 - core
    chip = (zh * 2 + inner % 2) * 16 + (inner // 8) * 4 + inner // 2 % 4
    number = outer * 32 + inner
    after, before = (number + 1) % 256, (number + 255) % 256
    sibling = device_of(chip, other)
    next_device = (after // 32, after % 32)
    last_device = (before // 32, before % 32)

    loads = []
    pairs = (
        (obj_hbm, obj),
        (probe_hbm, probe),
        (int_hbm, inten.at[core]),
        (base_hbm.at[core], base),
        (chip_turn_hbm, chip_turn),
        (col_chirp_hbm, col_chirp),
        (row_chirp_hbm, row_chirp),
        (first_hbm, first),
        (last_hbm, last),
        (last_back_hbm, last_back),
        (twiddle_hbm, twiddle),
        (first_back_hbm, first_back),
    )
    for slot, (source, target) in enumerate(pairs):
        copy = pltpu.make_async_copy(source, target, load_sem.at[slot])
        copy.start()
        loads.append(copy)

    barrier = pltpu.get_barrier_semaphore()
    greeted = [device_of(flip(chip, k << 4), core) for k in range(1, 8)]
    greeted += [device_of(flip(chip, k << 2), core) for k in range(1, 4)]
    greeted += [device_of(flip(chip, k), core) for k in range(1, 4)]
    greeted += [sibling, next_device, last_device]
    for device in greeted:
        pl.semaphore_signal(barrier, inc=1, device_id=device, device_id_type=MESH)

    rows_by, cols_by = row_off[0], col_off[0]
    tiles_by, lanes_by = cols_by // 128, cols_by % 128
    lane = lax.broadcasted_iota(jnp.int32, (8, 128), 1)
    sub = lax.broadcasted_iota(jnp.int32, (8, 128), 0)
    loads[0].wait()
    for part in range(2):

        def roll_step(step, carry, part=part):
            for inside in range(8):
                at = step * 8 + inside
                piece = obj[part, :, pl.ds(pl.multiple_of(at * 128, 128), 128)]
                moved = pltpu.roll(pltpu.roll(piece, lanes_by, 1), rows_by, 0)
                rolled[pl.ds(part * 64 + at, 8, stride=128), :] = moved
            return carry

        lax.fori_loop(0, 8, roll_step, 0)
    wide_lane = lax.broadcasted_iota(jnp.int32, (64, 128), 1)

    def tile_step(block, carry):
        at = pl.ds(pl.multiple_of(block * 64, 64), 64)
        moved = pltpu.roll(rolled[at, :], tiles_by, 0)
        rolled[at, :] = jnp.where(wide_lane < lanes_by, pltpu.roll(moved, 1, 0), moved)
        return carry

    lax.fori_loop(0, 16, tile_step, 0)
    arrived[pl.ds(896, 128), :] = jnp.zeros((128, 128), F32)

    pl.semaphore_wait(barrier, 16)

    shift = pltpu.make_async_remote_copy(
        src_ref=rolled.at[pl.ds(0, 896)],
        dst_ref=arrived.at[pl.ds(0, 896)],
        send_sem=shift_sem.at[0],
        recv_sem=shift_sem.at[1],
        device_id=next_device,
        device_id_type=MESH,
    )
    shift.start()
    loads[2].wait()
    share = pltpu.make_async_remote_copy(
        src_ref=inten.at[core],
        dst_ref=inten.at[core],
        send_sem=int_sem.at[0],
        recv_sem=int_sem.at[1],
        device_id=sibling,
        device_id_type=MESH,
    )
    share.start()

    loads[1].wait()

    def peak_step(step, best):
        for inside in range(8):
            at = pl.ds(pl.multiple_of((step * 8 + inside) * 128, 128), 128)
            real, imag = probe[0, :, at], probe[1, :, at]
            best = jnp.maximum(best, real * real + imag * imag)
        return best

    peak_own[0] = lax.fori_loop(0, 8, peak_step, jnp.zeros((8, 128), F32))

    def peak_line(source, target, sem, count, by):
        copies = []
        for k in range(1, count):
            copy = pltpu.make_async_remote_copy(
                src_ref=source,
                dst_ref=target.at[k - 1],
                send_sem=sem.at[k - 1],
                recv_sem=sem.at[count - 2 + k],
                device_id=device_of(flip(chip, k << by), core),
                device_id_type=MESH,
            )
            copy.start()
            copies.append(copy)
        return copies

    z_line = peak_line(peak_own.at[0], peak_z, z_sem, 8, 4)

    loads[3].wait()
    loads[4].wait()
    chip_lane = lax.broadcasted_iota(jnp.int32, (64, 128), 1) == chip
    turn_re = jnp.sum(jnp.where(chip_lane, chip_turn[0], 0.0), axis=1, keepdims=True)
    turn_im = jnp.sum(jnp.where(chip_lane, chip_turn[1], 0.0), axis=1, keepdims=True)
    for block in range(4):
        low, high = pl.ds(block * 128, 64), pl.ds(block * 128 + 64, 64)
        for_re, for_im = base[low, :], base[high, :]
        for at, value in (
            (low, for_re * turn_re + for_im * turn_im),
            (high, for_im * turn_re - for_re * turn_im),
        ):
            high_part, low_part = split(value)
            mixed[0, at, :] = high_part
            mixed[1, at, :] = low_part

    for copy in z_line:
        copy.wait_recv()
    best = peak_own[0]
    for k in range(7):
        best = jnp.maximum(best, peak_z[k])
    peak_own[1] = best
    y_line = peak_line(peak_own.at[1], peak_y, y_sem, 4, 2)

    share.wait_recv()
    for c in range(2):

        def spread_step(step, carry, c=c):
            for inside in range(8):
                at = step * 8 + inside
                piece = inten[c, :, pl.ds(pl.multiple_of(at * 128, 128), 128)]
                spread[pl.ds(c * 64 + at, 8, stride=128), :] = piece
            return carry

        lax.fori_loop(0, 8, spread_step, 0)
    for l in range(4):
        shades_out[pl.ds(l, 128, stride=8), :] = jnp.transpose(spread[pl.ds(l * 128, 128), :])

    for copy in y_line:
        copy.wait_recv()
    for k in range(3):
        best = jnp.maximum(best, peak_y[k])
    peak_own[2] = best
    x_line = peak_line(peak_own.at[2], peak_x, x_sem, 4, 0)
    for l in range(4, 8):
        shades_out[pl.ds(l, 128, stride=8), :] = jnp.transpose(spread[pl.ds(l * 128, 128), :])
    for copy in x_line:
        copy.wait_recv()
    for k in range(3):
        best = jnp.maximum(best, peak_x[k])
    peak_own[3] = best
    c_line = pltpu.make_async_remote_copy(
        src_ref=peak_own.at[3],
        dst_ref=peak_c,
        send_sem=c_sem.at[0],
        recv_sem=c_sem.at[1],
        device_id=sibling,
        device_id_type=MESH,
    )
    c_line.start()

    def shade_step(step, carry):
        target = flip(chip, 2 * step + core)
        pltpu.make_async_remote_copy(
            src_ref=tile(shades_out, target),
            dst_ref=shades_in.at[chip // 2, chip % 2],
            send_sem=shade_sem.at[0],
            recv_sem=shade_sem.at[1],
            device_id=device_of(target, core),
            device_id_type=MESH,
        ).start()
        return carry

    lax.fori_loop(1, 64, shade_step, 0)

    @pl.when(core == 1)
    def _():
        shade_step(0, 0)

    @pl.when(core == 0)
    def _():
        own = pltpu.make_async_copy(
            tile(shades_out, chip), shades_in.at[chip // 2, chip % 2], local_sem.at[0]
        )
        own.start()
        own.wait()

    for slot in (5, 6, 7):
        loads[slot].wait()
    number_lane = lax.broadcasted_iota(jnp.int32, (8, 256), 1) == number
    row_re = jnp.sum(jnp.where(number_lane, row_chirp[0], 0.0), axis=1, keepdims=True)
    row_im = jnp.sum(jnp.where(number_lane, row_chirp[1], 0.0), axis=1, keepdims=True)

    def chirp_at(at):
        col_re, col_im = col_chirp[0, :, at], col_chirp[1, :, at]
        return row_re * col_re - row_im * col_im, row_re * col_im + row_im * col_re

    shift.wait_recv()

    def wave_step(step, carry):
        for inside in range(8):
            index = step * 8 + inside
            at = pl.ds(pl.multiple_of(index * 128, 128), 128)
            views = []
            for part in range(2):
                rows = pl.ds(part * 64 + index, 8, stride=128)
                views.append(jnp.where(sub < rows_by, arrived[rows, :], rolled[rows, :]))
            probe_re, probe_im = probe[0, :, at], probe[1, :, at]
            real = probe_re * views[0] - probe_im * views[1]
            imag = probe_re * views[1] + probe_im * views[0]
            wave[0, :, at] = real
            wave[1, :, at] = imag
            chirp_re, chirp_im = chirp_at(at)
            real, imag = real * chirp_re - imag * chirp_im, real * chirp_im + imag * chirp_re
            even = jnp.where(lane < 64, real, pltpu.roll(imag, 64, 1))
            odd = jnp.where(lane < 64, pltpu.roll(real, 64, 1), imag)
            turned[pl.ds(index, 8, stride=128), :] = even
            turned[pl.ds(64 + index, 8, stride=128), :] = odd
        return carry

    lax.fori_loop(0, 8, wave_step, 0)

    def times_i(value):
        half = lax.broadcasted_iota(jnp.int32, value.shape, 1) < 64
        moved = pltpu.roll(value, 64, 1)
        return jnp.where(half, -moved, moved)

    def first_step(load, table, store):
        for pair in range(4):
            sides = []
            for row in (2 * pair, 2 * pair + 1):
                value = load(row)
                sides.append(jnp.concatenate([value, times_i(value)], axis=0))
            result = three(dot, (table[0], table[1]), split(jnp.concatenate(sides, axis=1)))
            store(2 * pair, result[:, :128])
            store(2 * pair + 1, result[:, 128:])

    def store_field(row, value):
        field_out[pl.ds(row, 128, stride=8), :] = value

    first_step(lambda row: turned[pl.ds(row * 128, 128), :], first, store_field)

    def send_all(source, target, sem):
        def send_step(k, carry):
            to = flip(chip, k)
            pltpu.make_async_remote_copy(
                src_ref=tile(source, to),
                dst_ref=tile(target, chip),
                send_sem=sem.at[0],
                recv_sem=sem.at[1],
                device_id=device_of(to, core),
                device_id_type=MESH,
            ).start()
            return carry

        lax.fori_loop(1, 128, send_step, 0)
        own = pltpu.make_async_copy(tile(source, chip), tile(target, chip), local_sem.at[0])
        own.start()
        own.wait()

    def all_of(source, target, sem, rows):
        return pltpu.make_async_remote_copy(
            src_ref=source.at[pl.ds(0, rows)],
            dst_ref=target.at[pl.ds(0, rows)],
            send_sem=sem.at[0],
            recv_sem=sem.at[1],
            device_id=sibling,
            device_id_type=MESH,
        )

    send_all(field_out, field_in, field_sem)

    @pl.when(core == 0)
    def _():
        all_of(shades_out, field_in, shade_sem, 504).wait()

    @pl.when(core == 1)
    def _():
        all_of(shades_out, field_in, shade_sem, 512).wait()

    mine = (chip + core) % 2
    hand_over = pltpu.make_async_remote_copy(
        src_ref=shades_in.at[:, mine],
        dst_ref=shades_in.at[:, mine],
        send_sem=pass_sem.at[0],
        recv_sem=pass_sem.at[1],
        device_id=sibling,
        device_id_type=MESH,
    )
    hand_over.start()
    hand_over.wait()
    group = lax.broadcasted_iota(jnp.int32, (256, 128), 1) // 32
    for c in range(2):
        shade = jnp.zeros((256, 128), F32)
        for digit in range(4):
            want = 2 * (digit % 2) + digit // 2
            by = (32 * (want - 2 * c - core) + 128) % 128
            part = shades_in[pl.ds(digit * 16, 16)].reshape(256, 128)
            shade = jnp.where(group == want, pltpu.roll(part, by, 1), shade)
        factor[c] = jnp.sqrt(shade)
    c_line.wait_recv()
    peak_ref[...] = jnp.maximum(best, peak_c[...])

    all_of(field_out, field_in, field_sem, 1016).wait()
    joined = jnp.concatenate([field_in[pl.ds(digit * 256, 256), :] for digit in range(4)], axis=1)
    joined = split(joined)
    mixed_table = (mixed[0], mixed[1])
    result = three(dot, joined, mixed_table)
    mixed_out[0] = result[:, 256:]
    mix = pltpu.make_async_remote_copy(
        src_ref=mixed_out.at[0],
        dst_ref=mixed_out.at[1],
        send_sem=mix_sem.at[0],
        recv_sem=mix_sem.at[1],
        device_id=sibling,
        device_id_type=MESH,
    )
    mix.start()
    kept = result[:, :256]
    loads[8].wait()
    loads[10].wait()
    mix.wait_recv()
    got = mixed_out[1]
    sign = jnp.where(core == 0, 1.0, -1.0).astype(F32)
    sums = (kept + got, (kept - got) * sign)
    data = []
    for k2 in range(2):
        real, imag = sums[k2][:, :128], sums[k2][:, 128:]
        turn_r, turn_i = twiddle[k2, 0], twiddle[k2, 1]
        data.append(
            jnp.concatenate([real * turn_r - imag * turn_i, real * turn_i + imag * turn_r], axis=0)
        )
    spectrum = three(dot, (last[0], last[1]), split(jnp.concatenate(data, axis=1)))
    data = []
    for k2 in range(2):
        real = spectrum[:256, k2 * 128 : (k2 + 1) * 128]
        imag = spectrum[256:, k2 * 128 : (k2 + 1) * 128]
        scale = factor[k2] / jnp.maximum(jnp.sqrt(real * real + imag * imag), FLOOR_LEVEL)
        data.append(jnp.concatenate([real * scale, imag * scale], axis=0))
    loads[9].wait()
    field = three(dot, (last_back[0], last_back[1]), split(jnp.concatenate(data, axis=1)))
    parts = []
    for k2 in range(2):
        real = field[:256, k2 * 128 : (k2 + 1) * 128]
        imag = field[256:, k2 * 128 : (k2 + 1) * 128]
        turn_r, turn_i = twiddle[k2, 0], twiddle[k2, 1]
        parts.append(
            jnp.concatenate([real * turn_r + imag * turn_i, imag * turn_r - real * turn_i], axis=1)
        )
    plus, minus = parts[0] + parts[1], parts[0] - parts[1]
    own_core = core == 0
    part_out[...] = jnp.where(own_core, minus, plus)
    swap = pltpu.make_async_remote_copy(
        src_ref=part_out,
        dst_ref=part_in,
        send_sem=part_sem.at[0],
        recv_sem=part_sem.at[1],
        device_id=sibling,
        device_id_type=MESH,
    )
    swap.start()
    own = jnp.where(own_core, plus, minus)
    swap.wait_recv()
    joined = split(jnp.concatenate([own, part_in[...]], axis=1))
    result = three(dot_t, joined, mixed_table)
    for digit in range(4):
        back_out[pl.ds(digit * 256, 256), :] = result[:, digit * 128 : (digit + 1) * 128]
    send_all(back_out, back_in, back_sem)

    loads[11].wait()
    all_of(back_out, back_in, back_sem, 1016).wait()

    def store_turned(row, value):
        turned[pl.ds(row * 128, 128), :] = value

    first_step(lambda row: back_in[pl.ds(row, 128, stride=8), :], first_back, store_turned)

    def last_step(step, carry):
        for inside in range(8):
            index = step * 8 + inside
            at = pl.ds(pl.multiple_of(index * 128, 128), 128)
            even = turned[pl.ds(index, 8, stride=128), :]
            odd = turned[pl.ds(64 + index, 8, stride=128), :]
            real = jnp.where(lane < 64, even, pltpu.roll(odd, 64, 1))
            imag = jnp.where(lane < 64, pltpu.roll(even, 64, 1), odd)
            chirp_re, chirp_im = chirp_at(at)
            step_re = real * chirp_re + imag * chirp_im - wave[0, :, at]
            step_im = imag * chirp_re - real * chirp_im - wave[1, :, at]
            probe_re, probe_im = probe[0, :, at], probe[1, :, at]
            out_ref[0, :, at] = probe_re * step_re + probe_im * step_im
            out_ref[1, :, at] = probe_re * step_im - probe_im * step_re
        return carry

    lax.fori_loop(0, 8, last_step, 0)

    shift.wait_send()
    share.wait_send()
    for copy in z_line + y_line + x_line:
        copy.wait_send()
    c_line.wait_send()
    mix.wait_send()
    swap.wait_send()


def body(object_field, probe, intensity, row_offset, col_offset):
    tables = make_tables()
    constants = [jnp.asarray(tables[name]) for name in TABLES]
    vmem, dma = pltpu.VMEM, pltpu.SemaphoreType.DMA
    anywhere = pl.BlockSpec(memory_space=pl.ANY)
    scalar = pl.BlockSpec(memory_space=pltpu.SMEM)
    inside = pl.BlockSpec(memory_space=pltpu.VMEM)
    state = vmem((1024, 128), F32)
    scratch = [
        vmem((2, 8, 8192), F32),
        vmem((2, 8, 8192), F32),
        vmem((2, 8, 8192), F32),
        vmem((2, 1, 8192), F32),
        vmem((2, 8, 256), F32),
        vmem((2, 128, 256), BF16),
        vmem((2, 128, 256), BF16),
        vmem((2, 64, 128), F32),
        vmem((512, 512), F32),
        vmem((2, 512, 512), BF16),
        vmem((2, 512, 512), BF16),
        vmem((2, 2, 256, 128), F32),
        state,
        state,
        vmem((2, 8, 8192), F32),
        state,
        state,
        state,
        vmem((2, 512, 512), BF16),
        vmem((2, 256, 256), F32),
        vmem((2, 256, 128), F32),
        state,
        state,
        vmem((64, 2, 8, 128), F32),
        state,
        state,
        vmem((256, 256), F32),
        vmem((256, 256), F32),
        vmem((4, 8, 128), F32),
        vmem((7, 8, 128), F32),
        vmem((3, 8, 128), F32),
        vmem((3, 8, 128), F32),
        vmem((8, 128), F32),
        dma((12,)),
        dma((2,)),
        dma((2,)),
        dma((14,)),
        dma((6,)),
        dma((6,)),
        dma((2,)),
        dma((2,)),
        dma((2,)),
        dma((2,)),
        dma((2,)),
        dma((2,)),
        dma((2,)),
        dma((1,)),
    ]
    step, peak = pl.pallas_call(
        kernel,
        out_shape=(
            jax.ShapeDtypeStruct(object_field.shape, F32),
            jax.ShapeDtypeStruct((8, 128), F32),
        ),
        in_specs=[scalar, scalar] + [anywhere] * (3 + len(constants)),
        out_specs=(inside, inside),
        scratch_shapes=scratch,
        compiler_params=pltpu.CompilerParams(
            collective_id=0, has_side_effects=True, vmem_limit_bytes=40 << 20
        ),
        cost_estimate=pl.CostEstimate(
            flops=2_000_000_000, bytes_accessed=8_000_000, transcendentals=200_000
        ),
    )(row_offset, col_offset, object_field, probe, intensity, *constants)
    return step / jnp.max(peak)


def solution(mesh):
    placed = (
        P(None, ("outer", "inner"), None),
        P(None, ("outer", "inner"), None),
        P(("outer", "inner"), None),
        P(),
        P(),
    )
    return jax.shard_map(
        body,
        mesh=mesh,
        in_specs=placed,
        out_specs=P(None, ("outer", "inner"), None),
        check_vma=False,
    )
```

profile of v0, /device:TPU:1, one launch (start us, length us, event | category | flops | bytes accessed | tf_op | source)
XLA Modules:
  0.0 91.7 jit_solution(105494917701416468)
XLA Ops:
  1.3 0.0 copy-start
  1.3 1.0 %copy-done = f32[2,8,8192]{2,1,0:T(8,128)S(1)} copy-done((f32[2,8,8192]{2,1,0:T(8,128)S(1)}, f32[2,8,8192]{2,1,0:T(8,128)}, u32[]{:S(2)}) %copy-start) | copy-done | bytes 524312
  2.3 0.0 copy-start.1
  2.3 1.0 %copy-done.1 = f32[2,8,8192]{2,1,0:T(8,128)S(1)} copy-done((f32[2,8,8192]{2,1,0:T(8,128)S(1)}, f32[2,8,8192]{2,1,0:T(8,128)}, u32[]{:S(2)}) %copy-start.1) | copy-done | bytes 524312
  3.4 0.0 copy-start.2
  3.4 0.9 %copy-done.2 = f32[8,8192]{1,0:T(8,128)S(1)} copy-done((f32[8,8192]{1,0:T(8,128)S(1)}, f32[8,8192]{1,0:T(8,128)}, u32[]{:S(2)}) %copy-start.2) | copy-done | bytes 262168
  4.3 0.0 copy-start.3
  4.3 1.6 %copy-done.3 = f32[2,512,512]{2,1,0:T(8,128)S(1)} copy-done((f32[2,512,512]{2,1,0:T(8,128)S(1)}, f32[2,512,512]{2,1,0:T(8,128)}, u32[]{:S(2)}) %copy-start.3) | copy-done | bytes 2097176
  5.9 0.0 copy-start.4
  5.9 1.2 %copy-done.4 = bf16[2,512,512]{2,1,0:T(8,128)(2,1)S(1)} copy-done((bf16[2,512,512]{2,1,0:T(8,128)(2,1)S(1)}, bf16[2,512,512]{2,1,0:T(8,128)(2,1)}, u32[]{:S(2)}) %copy-start.4) | copy-done | bytes 1048600
  7.1 0.0 copy-start.5
  7.2 1.2 %copy-done.5 = bf16[2,512,512]{2,1,0:T(8,128)(2,1)S(1)} copy-done((bf16[2,512,512]{2,1,0:T(8,128)(2,1)S(1)}, bf16[2,512,512]{2,1,0:T(8,128)(2,1)}, u32[]{:S(2)}) %copy-start.5) | copy-done | bytes 1048600
  8.4 0.0 copy-start.6
  8.4 1.0 %copy-done.6 = f32[2,2,256,128]{3,2,1,0:T(8,128)S(1)} copy-done((f32[2,2,256,128]{3,2,1,0:T(8,128)S(1)}, f32[2,2,256,128]{3,2,1,0:T(8,128)}, u32[]{:S(2)}) %copy-start.6) | copy-done | bytes 524312
  9.4 0.0 copy-start.7
  9.4 0.9 copy-done.7
  10.3 0.0 copy-start.8
  10.3 0.9 copy-done.8
  11.2 0.8 copy-done.9
  12.1 0.8 copy-done.10
  12.9 0.7 copy-done.11
  13.6 75.9 %shard_map.136 = (f32[2,8,8192]{2,1,0:T(8,128)S(1)}, f32[8,128]{1,0:T(8,128)S(1)}) custom-call(s32[1]{0:T(128)S(6)} %copy.15.row_off, s32[1]{0:T(128)S(6)} %copy.16.col_off, f32[2,8,8192]{2,1,0:T(8,128)S(1)} %copy-done, f32[2,8,8192]{2,1,0:T(8,128)S(1)} %copy-done.1, f32[8,8192]{1,0:T(8,128)S(1)} %copy-done.2, f32[2,1,8192]{2,1,0:T(1,128)S(1)} %copy-done.10, ...), custom_call_target="tpu_custom_call" | custom-call | flops 2000000000 | bytes 8000000 | tf_op jit(solution)/shard_map/pallas_call | solution.py:664
  89.6 0.6 reduce_max.9
  90.2 1.5 %broadcast_divide_fusion = f32[2,8,8192]{2,1,0:T(8,128)} fusion(f32[2,8,8192]{2,1,0:T(8,128)S(1)} %get-tuple-element.7, f32[]{:T(128)} %reduce_max.9), kind=kLoop, calls=%fused_computation | loop fusion | flops 131072 | bytes 1048580 | tf_op jit(solution)/shard_map/div | solution.py:680
  (3 shorter events, 0.0 us)
Async XLA Ops:
  1.3 1.0 %copy-start = (f32[2,8,8192]{2,1,0:T(8,128)S(1)}, f32[2,8,8192]{2,1,0:T(8,128)}, u32[]{:S(2)}) copy-start(f32[2,8,8192]{2,1,0:T(8,128)} %obj_hbm.1) | copy-start | bytes 1572868
  2.3 1.0 %copy-start.1 = (f32[2,8,8192]{2,1,0:T(8,128)S(1)}, f32[2,8,8192]{2,1,0:T(8,128)}, u32[]{:S(2)}) copy-start(f32[2,8,8192]{2,1,0:T(8,128)} %probe_hbm.1) | copy-start | bytes 1572868
  3.4 0.9 %copy-start.2 = (f32[8,8192]{1,0:T(8,128)S(1)}, f32[8,8192]{1,0:T(8,128)}, u32[]{:S(2)}) copy-start(f32[8,8192]{1,0:T(8,128)} %int_hbm.1) | copy-start | bytes 786436
  4.3 1.6 %copy-start.3 = (f32[2,512,512]{2,1,0:T(8,128)S(1)}, f32[2,512,512]{2,1,0:T(8,128)}, u32[]{:S(2)}) copy-start(f32[2,512,512]{2,1,0:T(8,128)} %constant.25.clone.base_hbm) | copy-start | bytes 6291460
  5.9 1.2 %copy-start.4 = (bf16[2,512,512]{2,1,0:T(8,128)(2,1)S(1)}, bf16[2,512,512]{2,1,0:T(8,128)(2,1)}, u32[]{:S(2)}) copy-start(bf16[2,512,512]{2,1,0:T(8,128)(2,1)} %constant.27.clone.last_back_hbm) | copy-start | bytes 3145732
  7.1 1.2 %copy-start.5 = (bf16[2,512,512]{2,1,0:T(8,128)(2,1)S(1)}, bf16[2,512,512]{2,1,0:T(8,128)(2,1)}, u32[]{:S(2)}) copy-start(bf16[2,512,512]{2,1,0:T(8,128)(2,1)} %constant.26.clone.last_hbm) | copy-start | bytes 3145732
  8.4 1.0 %copy-start.6 = (f32[2,2,256,128]{3,2,1,0:T(8,128)S(1)}, f32[2,2,256,128]{3,2,1,0:T(8,128)}, u32[]{:S(2)}) copy-start(f32[2,2,256,128]{3,2,1,0:T(8,128)} %constant.28.clone.twiddle_hbm) | copy-start | bytes 1572868
  9.4 0.9 copy-start.7
  10.3 0.9 copy-start.8
  11.2 0.8 copy-start.9
  12.1 0.8 copy-start.10
  12.9 0.7 copy-start.11
where the time goes:
time: 92.2 us; the launch traced here: 91.7 us
  Pallas kernels  75.9 us (82%)
  local copies, waits for them, and re-layouts  12.3 us (13%)
  other arithmetic  2.09 us (2%)
  between operations  1.33 us (1%)
    pallas_call x1, Pallas kernels, body(): pl.pallas_call(kernel, out_shape=(jax.ShapeDtypeStruct(object_field.shape...  75.9 us
    unnamed x24, local copies, waits for them, and re-layouts  12.3 us

commit v1 on v0

v1 whole, which is shorter than its diff:
```python
import math

import jax
import jax.numpy as jnp
import numpy as np
from jax import lax
from jax.experimental import pallas as pl
from jax.experimental.pallas import tpu as pltpu
from jax.sharding import PartitionSpec as P

FLOOR_LEVEL = 0.1
EARLY = 3
MESH = pl.DeviceIdType.MESH
CHIPS = 128
F32 = jnp.float32
BF16 = jnp.bfloat16


def split_table(table):
    table = np.asarray(table, np.float64).astype(np.float32)
    high = table.astype(jnp.bfloat16)
    low = (table - high.astype(np.float32)).astype(jnp.bfloat16)
    return np.stack([high, low])


def turn(numerator, modulus):
    angle = -2.0 * np.pi * (np.asarray(numerator) % modulus) / modulus
    return np.exp(1j * angle)


def expanded(table):
    return np.block([[table.real, table.imag], [-table.imag, table.real]])


def make_tables():
    tables = {}
    col = np.arange(8192, dtype=np.int64) - 4096
    col_phase = np.pi / 8192 * (col * col % 16384)
    tables["col_chirp"] = np.stack([np.cos(col_phase), np.sin(col_phase)]).reshape(2, 1, 8192).astype(np.float32)
    row = np.arange(2048, dtype=np.int64) - 1024
    row_phase = (np.pi / 2048 * (row * row % 4096)).reshape(256, 8).T
    tables["row_chirp"] = np.stack([np.cos(row_phase), np.sin(row_phase)]).astype(np.float32)
    order = np.concatenate([2 * np.arange(64), 2 * np.arange(64) + 1])
    first = turn(np.arange(128)[:, None] * order[None, :], 128)
    tables["first"] = split_table(np.concatenate([first.real, first.imag], axis=1))
    back = np.conj(first).T
    tables["first_back"] = split_table(np.concatenate([back.real, back.imag], axis=1))
    chip_turn = turn(np.arange(64)[:, None] * np.arange(128)[None, :], 8192)
    tables["chip_turn"] = np.stack([chip_turn.real, chip_turn.imag]).astype(np.float32)
    base = []
    for core in range(2):
        blocks = []
        for zh in range(4):
            halves = []
            for half in range(2):
                q = 32 * (core if half == 0 else 1 - core) + np.arange(32)
                klow = np.arange(4)
                m = np.arange(64)
                power = (
                    m[:, None, None] * q[None, None, :] * 8
                    + zh * klow[None, :, None] * 128
                    + core * klow[None, :, None] * 64
                )
                halves.append(expanded(turn(power, 512).reshape(64, 128)))
            blocks.append(np.concatenate(halves, axis=1))
        base.append(np.concatenate(blocks, axis=0))
    tables["base"] = np.stack(base).astype(np.float32)
    index = np.arange(256)
    y, zl, x, l = index // 64, index // 32 % 2, index // 8 % 4, index % 8
    n = 64 * y + 16 * x + 8 * zl + l
    last = turn(n[:, None] * n[None, :], 256)
    for name, sign in (("last", 1.0), ("last_back", -1.0)):
        whole = np.block([[last.real, -sign * last.imag], [sign * last.imag, last.real]])
        blocks = whole.reshape(2, 4, 64, 512).transpose(1, 0, 2, 3).reshape(4, 128, 512)
        tables[name] = split_table(blocks)
    klow = np.arange(128) // 32
    twiddle = np.stack([turn(n[:, None] * (klow[None, :] + 4 * k2), 2048) for k2 in range(2)]) / 4096.0
    tables["twiddle"] = np.stack([twiddle.real, twiddle.imag], axis=1).astype(np.float32)
    return tables


TABLES = (
    "col_chirp",
    "row_chirp",
    "first",
    "first_back",
    "chip_turn",
    "base",
    "last",
    "last_back",
    "twiddle",
)


def split(value):
    high = value.astype(BF16)
    low = (value - high.astype(F32)).astype(BF16)
    return high, low


def dot(left, right):
    return jnp.dot(left, right, preferred_element_type=F32)


def dot_t(left, right):
    return lax.dot_general(left, right, (((1,), (1,)), ((), ())), preferred_element_type=F32)


def three(op, left, right):
    return op(left[0], right[0]) + (op(left[0], right[1]) + op(left[1], right[0]))


def device_of(chip, core):
    z = chip // 4 % 8
    return (z // 2) * 2 + core, (chip // 32) * 8 + (chip % 4) * 2 + z % 2


def flip(chip, offset):
    return chip ^ offset


def tile(ref, index):
    return ref.at[pl.ds(pl.multiple_of(index * 8, 8), 8)]


def kernel(
    row_off,
    col_off,
    obj_hbm,
    probe_hbm,
    int_hbm,
    col_chirp_hbm,
    row_chirp_hbm,
    first_hbm,
    first_back_hbm,
    chip_turn_hbm,
    base_hbm,
    last_hbm,
    last_back_hbm,
    twiddle_hbm,
    out_ref,
    obj,
    probe,
    inten,
    col_chirp,
    row_chirp,
    first,
    first_back,
    chip_turn,
    base,
    last,
    last_back,
    twiddle,
    rolled,
    arrived,
    wave,
    turned,
    field_out,
    field_in,
    mixed,
    mix_out,
    mix_in,
    mix_kept,
    data,
    again,
    factor,
    spread,
    shades_out,
    shades_in,
    back_out,
    back_in,
    part_out,
    part_in,
    part_own,
    peak_own,
    peak_z,
    peak_y,
    peak_x,
    peak_c,
    load_sem,
    shift_sem,
    int_sem,
    z_sem,
    y_sem,
    x_sem,
    c_sem,
    shade_sem,
    pass_sem,
    field_sem,
    mix_sem,
    part_sem,
    back_sem,
    local_sem,
    gates,
):
    outer, inner = lax.axis_index("outer"), lax.axis_index("inner")
    zh, core = outer // 2, outer % 2
    other = 1 - core
    z, y, x = zh * 2 + inner % 2, inner // 8, inner // 2 % 4
    chip = y * 32 + z * 4 + x
    number = outer * 32 + inner
    after, before = (number + 1) % 256, (number + 255) % 256
    sibling = device_of(chip, other)
    next_device = (after // 32, after % 32)
    last_device = (before // 32, before % 32)

    loads = []
    pairs = (
        (obj_hbm, obj),
        (probe_hbm, probe),
        (int_hbm, inten.at[core]),
        (base_hbm.at[core], base),
        (chip_turn_hbm, chip_turn),
        (col_chirp_hbm, col_chirp),
        (row_chirp_hbm, row_chirp),
        (first_hbm, first),
        (last_hbm, last),
        (last_back_hbm, last_back),
        (twiddle_hbm, twiddle),
        (first_back_hbm, first_back),
    )
    for slot, (source, target) in enumerate(pairs):
        copy = pltpu.make_async_copy(source, target, load_sem.at[slot])
        copy.start()
        loads.append(copy)

    barrier = pltpu.get_barrier_semaphore()

    def at_chip(dz, dy, dx):
        to = (y + dy + 4) % 4 * 32 + (z + dz + 8) % 8 * 4 + (x + dx + 4) % 4
        return device_of(to, core)

    around = [at_chip(*by) for by in ((1, 0, 0), (-1, 0, 0), (0, 1, 0), (0, -1, 0), (0, 0, 1), (0, 0, -1))]
    greeted = around + [sibling, next_device, last_device]
    for device in greeted:
        pl.semaphore_signal(barrier, inc=1, device_id=device, device_id_type=MESH)

    def tell(gate, devices):
        for device in devices:
            pl.semaphore_signal(gate, inc=1, device_id=device, device_id_type=MESH)


    rows_by, cols_by = row_off[0], col_off[0]
    tiles_by, lanes_by = cols_by // 128, cols_by % 128
    lane = lax.broadcasted_iota(jnp.int32, (8, 128), 1)
    sub = lax.broadcasted_iota(jnp.int32, (8, 128), 0)
    loads[0].wait()
    for part in range(2):
        for row in (7,):
            arrived[pl.ds(part * 512 + row * 64, 64), :] = jnp.zeros((64, 128), F32)
    wide_lane = lax.broadcasted_iota(jnp.int32, (64, 128), 1)
    shifts = []
    for part in range(2):

        def roll_step(step, carry, part=part):
            for inside in range(8):
                at = step * 8 + inside
                piece = obj[part, :, pl.ds(pl.multiple_of(at * 128, 128), 128)]
                moved = pltpu.roll(pltpu.roll(piece, lanes_by, 1), rows_by, 0)
                rolled[pl.ds(part * 512 + at, 8, stride=64), :] = moved
            return carry

        def tile_step(row, carry, part=part):
            at = pl.ds(pl.multiple_of(part * 512 + row * 64, 64), 64)
            moved = pltpu.roll(rolled[at, :], tiles_by, 0)
            rolled[at, :] = jnp.where(wide_lane < lanes_by, pltpu.roll(moved, 1, 0), moved)
            return carry

        lax.fori_loop(0, 8, roll_step, 0)
        lax.fori_loop(0, 8, tile_step, 0)
        if part == 0:
            pl.semaphore_wait(barrier, 9)
            tell(gates.at[0], around)
        shift = pltpu.make_async_remote_copy(
            src_ref=rolled.at[pl.ds(part * 512, 448)],
            dst_ref=arrived.at[pl.ds(part * 512, 448)],
            send_sem=shift_sem.at[part],
            recv_sem=shift_sem.at[2 + part],
            device_id=next_device,
            device_id_type=MESH,
        )
        shift.start()
        shifts.append(shift)
    loads[2].wait()
    share = pltpu.make_async_remote_copy(
        src_ref=inten.at[core],
        dst_ref=inten.at[core],
        send_sem=int_sem.at[0],
        recv_sem=int_sem.at[1],
        device_id=sibling,
        device_id_type=MESH,
    )
    share.start()
    pl.semaphore_wait(gates.at[0], 6)
    tell(gates.at[1], [at_chip(2, 0, 0), at_chip(-2, 0, 0)])

    loads[1].wait()

    def peak_step(step, best):
        for inside in range(8):
            at = pl.ds(pl.multiple_of((step * 8 + inside) * 128, 128), 128)
            real, imag = probe[0, :, at], probe[1, :, at]
            best = jnp.maximum(best, real * real + imag * imag)
        return best

    peak_own[0] = lax.fori_loop(0, 8, peak_step, jnp.zeros((8, 128), F32))

    pl.semaphore_wait(gates.at[1], 2)
    tell(gates.at[2], [device_of(flip(chip, k << 5), core) for k in range(1, 4)])
    loads[3].wait()
    loads[4].wait()
    chip_lane = lax.broadcasted_iota(jnp.int32, (64, 128), 1) == chip
    turn_re = jnp.sum(jnp.where(chip_lane, chip_turn[0], 0.0), axis=1, keepdims=True)
    turn_im = jnp.sum(jnp.where(chip_lane, chip_turn[1], 0.0), axis=1, keepdims=True)
    for block in range(4):
        low, high = pl.ds(block * 128, 64), pl.ds(block * 128 + 64, 64)
        for_re, for_im = base[low, :], base[high, :]
        for at, value in (
            (low, for_re * turn_re + for_im * turn_im),
            (high, for_im * turn_re - for_re * turn_im),
        ):
            high_part, low_part = split(value)
            mixed[0, at, :] = high_part
            mixed[1, at, :] = low_part

    pl.semaphore_wait(gates.at[2], 3)
    tell(gates.at[3], [device_of(flip(chip, k), core) for k in range(1, 4)])
    share.wait_recv()
    for c in range(2):

        def spread_step(step, carry, c=c):
            for inside in range(8):
                at = step * 8 + inside
                piece = inten[c, :, pl.ds(pl.multiple_of(at * 128, 128), 128)]
                spread[pl.ds(c * 64 + at, 8, stride=128), :] = piece
            return carry

        lax.fori_loop(0, 8, spread_step, 0)
    for l in range(4):
        shades_out[pl.ds(l, 128, stride=8), :] = jnp.transpose(spread[pl.ds(l * 128, 128), :])

    for l in range(4, 8):
        shades_out[pl.ds(l, 128, stride=8), :] = jnp.transpose(spread[pl.ds(l * 128, 128), :])
    pl.semaphore_wait(gates.at[3], 3)

    def send_shades(group):
        def shade_step(step, carry):
            target = flip(chip, group * 32 + step % 8 * 4 + step // 8 * 2 + core)
            pltpu.make_async_remote_copy(
                src_ref=tile(shades_out, target),
                dst_ref=shades_in.at[chip // 2, chip % 2],
                send_sem=shade_sem.at[0],
                recv_sem=shade_sem.at[1 + group],
                device_id=device_of(target, core),
                device_id_type=MESH,
            ).start()
            return carry

        lax.fori_loop(1 if group == 0 else 0, 16, shade_step, 0)
        if group == 0:

            @pl.when(core == 1)
            def _():
                shade_step(0, 0)

            @pl.when(core == 0)
            def _():
                own = pltpu.make_async_copy(
                    tile(shades_out, chip), shades_in.at[chip // 2, chip % 2], local_sem.at[0]
                )
                own.start()
                own.wait()

    for group in range(EARLY):
        send_shades(group)

    for slot in (5, 6, 7):
        loads[slot].wait()
    number_lane = lax.broadcasted_iota(jnp.int32, (8, 256), 1) == number
    row_re = jnp.sum(jnp.where(number_lane, row_chirp[0], 0.0), axis=1, keepdims=True)
    row_im = jnp.sum(jnp.where(number_lane, row_chirp[1], 0.0), axis=1, keepdims=True)

    def chirp_at(at):
        col_re, col_im = col_chirp[0, :, at], col_chirp[1, :, at]
        return row_re * col_re - row_im * col_im, row_re * col_im + row_im * col_re

    for shift in shifts:
        shift.wait_recv()

    def wave_step(step, carry):
        for inside in range(8):
            index = step * 8 + inside
            at = pl.ds(pl.multiple_of(index * 128, 128), 128)
            views = []
            for part in range(2):
                rows = pl.ds(part * 512 + index, 8, stride=64)
                views.append(jnp.where(sub < rows_by, arrived[rows, :], rolled[rows, :]))
            probe_re, probe_im = probe[0, :, at], probe[1, :, at]
            real = probe_re * views[0] - probe_im * views[1]
            imag = probe_re * views[1] + probe_im * views[0]
            wave[0, :, at] = real
            wave[1, :, at] = imag
            chirp_re, chirp_im = chirp_at(at)
            real, imag = real * chirp_re - imag * chirp_im, real * chirp_im + imag * chirp_re
            even = jnp.where(lane < 64, real, pltpu.roll(imag, 64, 1))
            odd = jnp.where(lane < 64, pltpu.roll(real, 64, 1), imag)
            turned[pl.ds(index, 8, stride=128), :] = even
            turned[pl.ds(64 + index, 8, stride=128), :] = odd
        return carry

    lax.fori_loop(0, 8, wave_step, 0)

    def times_i(value):
        half = lax.broadcasted_iota(jnp.int32, value.shape, 1) < 64
        moved = pltpu.roll(value, 64, 1)
        return jnp.where(half, -moved, moved)

    def first_step(load, table, store):
        for pair in range(4):
            sides = []
            for row in (2 * pair, 2 * pair + 1):
                value = load(row)
                sides.append(jnp.concatenate([value, times_i(value)], axis=0))
            result = three(dot, (table[0], table[1]), split(jnp.concatenate(sides, axis=1)))
            store(2 * pair, result[:, :128])
            store(2 * pair + 1, result[:, 128:])

    def store_field(row, value):
        field_out[pl.ds(row, 128, stride=8), :] = value

    first_step(lambda row: turned[pl.ds(row * 128, 128), :], first, store_field)

    def send_group(source, target, sem, group):
        def send_step(step, carry):
            to = flip(chip, group * 32 + step % 8 * 4 + step // 8)
            pltpu.make_async_remote_copy(
                src_ref=tile(source, to),
                dst_ref=tile(target, chip),
                send_sem=sem.at[0],
                recv_sem=sem.at[1 + group],
                device_id=device_of(to, core),
                device_id_type=MESH,
            ).start()
            return carry

        lax.fori_loop(1 if group == 0 else 0, 32, send_step, 0)
        if group == 0:
            own = pltpu.make_async_copy(tile(source, chip), tile(target, chip), local_sem.at[0])
            own.start()
            own.wait()

    def all_of(source, target, sem, rows, group=0):
        return pltpu.make_async_remote_copy(
            src_ref=source.at[pl.ds(0, rows)],
            dst_ref=target.at[pl.ds(0, rows)],
            send_sem=sem.at[0],
            recv_sem=sem.at[1 + group],
            device_id=sibling,
            device_id_type=MESH,
        )

    def got_group(source, target, sem, group):
        all_of(source, target, sem, 248 if group == 0 else 256, group).wait_recv()

    for group in range(4):
        send_group(field_out, field_in, field_sem, group)
    for group in range(EARLY, 4):
        send_shades(group)

    def peak_line(source, target, sem, count, by):
        copies = []
        for k in range(1, count):
            copy = pltpu.make_async_remote_copy(
                src_ref=source,
                dst_ref=target.at[k - 1],
                send_sem=sem.at[k - 1],
                recv_sem=sem.at[count - 2 + k],
                device_id=device_of(flip(chip, k << by), core),
                device_id_type=MESH,
            )
            copy.start()
            copies.append(copy)
        return copies

    z_line = peak_line(peak_own.at[0], peak_z, z_sem, 8, 2)


    mine = (chip + core) % 2

    def pass_shades(group):
        if group == 0:

            @pl.when(core == 0)
            def _():
                all_of(shades_out, field_in, shade_sem, 120, group).wait_recv()

            @pl.when(core == 1)
            def _():
                all_of(shades_out, field_in, shade_sem, 128, group).wait_recv()

        else:
            all_of(shades_out, field_in, shade_sem, 128, group).wait_recv()
        block = pl.ds((y ^ group) * 16, 16)
        copy = pltpu.make_async_remote_copy(
            src_ref=shades_in.at[block, mine],
            dst_ref=shades_in.at[block, mine],
            send_sem=pass_sem.at[group],
            recv_sem=pass_sem.at[4 + group],
            device_id=sibling,
            device_id_type=MESH,
        )
        copy.start()
        return copy

    lane_group = lax.broadcasted_iota(jnp.int32, (64, 128), 1) // 32

    def make_factor(group):
        for c in range(2):
            shade = jnp.zeros((64, 128), F32)
            for digit in range(4):
                want = 2 * (digit % 2) + digit // 2
                by = (32 * (want - 2 * c - core) + 128) % 128
                part = shades_in[pl.ds((y ^ group) * 16 + digit * 4, 4)].reshape(64, 128)
                shade = jnp.where(lane_group == want, pltpu.roll(part, by, 1), shade)
            factor[c, pl.ds(pl.multiple_of((y ^ group) * 64, 64), 64), :] = jnp.sqrt(shade)

    passes = [pass_shades(group) for group in range(EARLY)]
    for group in range(EARLY):
        passes[group].wait()
        make_factor(group)

    sent_half = (mixed.at[0, :, pl.ds(256, 256)], mixed.at[1, :, pl.ds(256, 256)])
    kept_half = (mixed.at[0, :, pl.ds(0, 256)], mixed.at[1, :, pl.ds(0, 256)])
    mixes = []
    sign = jnp.where(core == 0, 1.0, -1.0).astype(F32)
    loads[8].wait()
    loads[10].wait()

    def prepare(group):
        mixes[group].wait_recv()
        here = y ^ group
        rows = pl.ds(pl.multiple_of(here * 64, 64), 64)
        kept, got = mix_kept[rows, :], mix_in[rows, :]
        for k2, total in enumerate((kept + got, (kept - got) * sign)):
            real, imag = total[:, :128], total[:, 128:]
            turn_r, turn_i = twiddle[k2, 0, rows, :], twiddle[k2, 1, rows, :]
            lanes = pl.ds(k2 * 128, 128)
            for ri, value in enumerate(
                (real * turn_r - imag * turn_i, real * turn_i + imag * turn_r)
            ):
                at = pl.ds(pl.multiple_of(ri * 256 + here * 64, 64), 64)
                high_part, low_part = split(value)
                data[0, at, lanes] = high_part
                data[1, at, lanes] = low_part

    for group in range(4):
        got_group(field_out, field_in, field_sem, group)
        here = y ^ group
        pieces = [field_in[pl.ds(pl.multiple_of(here * 256 + digit * 64, 64), 64), :] for digit in range(4)]
        joined = split(jnp.concatenate(pieces, axis=1))
        rows = pl.ds(pl.multiple_of(here * 64, 64), 64)
        mix_out[rows, :] = three(dot, joined, (sent_half[0][...], sent_half[1][...]))
        mix = pltpu.make_async_remote_copy(
            src_ref=mix_out.at[rows],
            dst_ref=mix_in.at[rows],
            send_sem=mix_sem.at[group],
            recv_sem=mix_sem.at[4 + group],
            device_id=sibling,
            device_id_type=MESH,
        )
        mix.start()
        mixes.append(mix)
        mix_kept[rows, :] = three(dot, joined, (kept_half[0][...], kept_half[1][...]))
        if group > 0:
            prepare(group - 1)
    for copy in z_line:
        copy.wait_recv()
    best = peak_own[0]
    for k in range(7):
        best = jnp.maximum(best, peak_z[k])
    peak_own[1] = best
    y_line = peak_line(peak_own.at[1], peak_y, y_sem, 4, 5)
    late = [pass_shades(group) for group in range(EARLY, 4)]
    prepare(3)
    for group in range(EARLY, 4):
        late[group - EARLY].wait()
        make_factor(group)
    for block in range(4):
        value = three(dot, (last[0, block], last[1, block]), (data[0], data[1]))
        rows = pl.ds(block * 64, 64)
        for k2 in range(2):
            lanes = pl.ds(k2 * 128, 128)
            real = value[:64, k2 * 128 : (k2 + 1) * 128]
            imag = value[64:, k2 * 128 : (k2 + 1) * 128]
            size = jnp.sqrt(real * real + imag * imag)
            scale = factor[k2, rows, :] / jnp.maximum(size, FLOOR_LEVEL)
            for ri, part in enumerate((real * scale, imag * scale)):
                high_part, low_part = split(part)
                again[0, pl.ds(ri * 256 + block * 64, 64), lanes] = high_part
                again[1, pl.ds(ri * 256 + block * 64, 64), lanes] = low_part
    loads[9].wait()
    own_core = core == 0
    swaps = []
    for half in range(2):
        for group in (2 * half, 2 * half + 1):
            here = y ^ group
            rows = pl.ds(pl.multiple_of(here * 64, 64), 64)
            value = three(dot, (last_back[0, here], last_back[1, here]), (again[0], again[1]))
            parts = []
            for k2 in range(2):
                real = value[:64, k2 * 128 : (k2 + 1) * 128]
                imag = value[64:, k2 * 128 : (k2 + 1) * 128]
                turn_r, turn_i = twiddle[k2, 0, rows, :], twiddle[k2, 1, rows, :]
                parts.append(
                    jnp.concatenate(
                        [real * turn_r + imag * turn_i, imag * turn_r - real * turn_i], axis=1
                    )
                )
            plus, minus = parts[0] + parts[1], parts[0] - parts[1]
            part_out[rows, :] = jnp.where(own_core, minus, plus)
            part_own[rows, :] = jnp.where(own_core, plus, minus)
        rows = pl.ds(pl.multiple_of((y // 2 ^ half) * 128, 128), 128)
        swap = pltpu.make_async_remote_copy(
            src_ref=part_out.at[rows],
            dst_ref=part_in.at[rows],
            send_sem=part_sem.at[half],
            recv_sem=part_sem.at[2 + half],
            device_id=sibling,
            device_id_type=MESH,
        )
        swap.start()
        swaps.append(swap)
    for copy in y_line:
        copy.wait_recv()
    for k in range(3):
        best = jnp.maximum(best, peak_y[k])
    peak_own[2] = best
    x_line = peak_line(peak_own.at[2], peak_x, x_sem, 4, 0)
    for half in range(2):
        swaps[half].wait_recv()
        rows = pl.ds(pl.multiple_of((y // 2 ^ half) * 128, 128), 128)
        joined = split(jnp.concatenate([part_own[rows, :], part_in[rows, :]], axis=1))
        result = three(dot_t, joined, (mixed[0], mixed[1]))
        for low in range(2):
            for digit in range(4):
                at = pl.multiple_of((y // 2 ^ half) * 512 + low * 256 + digit * 64, 64)
                back_out[pl.ds(at, 64), :] = result[low * 64 : (low + 1) * 64, digit * 128 : (digit + 1) * 128]
        for group in (2 * half, 2 * half + 1):
            send_group(back_out, back_in, back_sem, group)
    for copy in x_line:
        copy.wait_recv()
    for k in range(3):
        best = jnp.maximum(best, peak_x[k])
    peak_own[3] = best
    c_line = pltpu.make_async_remote_copy(
        src_ref=peak_own.at[3],
        dst_ref=peak_c,
        send_sem=c_sem.at[0],
        recv_sem=c_sem.at[1],
        device_id=sibling,
        device_id_type=MESH,
    )
    c_line.start()
    c_line.wait_recv()
    gain = 1.0 / jnp.max(jnp.maximum(best, peak_c[...]))

    loads[11].wait()
    for group in range(4):
        got_group(back_out, back_in, back_sem, group)

    def store_turned(row, value):
        turned[pl.ds(row * 128, 128), :] = value

    first_step(lambda row: back_in[pl.ds(row, 128, stride=8), :], first_back, store_turned)

    def last_step(step, carry):
        for inside in range(8):
            index = step * 8 + inside
            at = pl.ds(pl.multiple_of(index * 128, 128), 128)
            even = turned[pl.ds(index, 8, stride=128), :]
            odd = turned[pl.ds(64 + index, 8, stride=128), :]
            real = jnp.where(lane < 64, even, pltpu.roll(odd, 64, 1))
            imag = jnp.where(lane < 64, pltpu.roll(even, 64, 1), odd)
            chirp_re, chirp_im = chirp_at(at)
            step_re = real * chirp_re + imag * chirp_im - wave[0, :, at]
            step_im = imag * chirp_re - real * chirp_im - wave[1, :, at]
            probe_re, probe_im = probe[0, :, at], probe[1, :, at]
            out_ref[0, :, at] = (probe_re * step_re + probe_im * step_im) * gain
            out_ref[1, :, at] = (probe_re * step_im - probe_im * step_re) * gain
        return carry

    lax.fori_loop(0, 8, last_step, 0)

    for shift in shifts:
        shift.wait_send()
    share.wait_send()
    for copy in z_line + y_line + x_line + mixes + swaps:
        copy.wait_send()
    c_line.wait_send()
    all_of(field_out, field_in, field_sem, 1016).wait_send()
    all_of(back_out, back_in, back_sem, 1016).wait_send()

    @pl.when(core == 0)
    def _():
        all_of(shades_out, field_in, shade_sem, 504).wait_send()

    @pl.when(core == 1)
    def _():
        all_of(shades_out, field_in, shade_sem, 512).wait_send()


def body(object_field, probe, intensity, row_offset, col_offset):
    tables = make_tables()
    constants = [jnp.asarray(tables[name]) for name in TABLES]
    vmem, dma = pltpu.VMEM, pltpu.SemaphoreType.DMA
    anywhere = pl.BlockSpec(memory_space=pltpu.HBM)
    scalar = pl.BlockSpec(memory_space=pltpu.SMEM)
    inside = pl.BlockSpec(memory_space=pltpu.VMEM)
    state = vmem((1024, 128), F32)
    scratch = [
        vmem((2, 8, 8192), F32),
        vmem((2, 8, 8192), F32),
        vmem((2, 8, 8192), F32),
        vmem((2, 1, 8192), F32),
        vmem((2, 8, 256), F32),
        vmem((2, 128, 256), BF16),
        vmem((2, 128, 256), BF16),
        vmem((2, 64, 128), F32),
        vmem((512, 512), F32),
        vmem((2, 4, 128, 512), BF16),
        vmem((2, 4, 128, 512), BF16),
        vmem((2, 2, 256, 128), F32),
        state,
        state,
        vmem((2, 8, 8192), F32),
        state,
        state,
        state,
        vmem((2, 512, 512), BF16),
        vmem((256, 256), F32),
        vmem((256, 256), F32),
        vmem((256, 256), F32),
        vmem((2, 512, 256), BF16),
        vmem((2, 512, 256), BF16),
        vmem((2, 256, 128), F32),
        state,
        state,
        vmem((64, 2, 8, 128), F32),
        state,
        state,
        vmem((256, 256), F32),
        vmem((256, 256), F32),
        vmem((256, 256), F32),
        vmem((4, 8, 128), F32),
        vmem((7, 8, 128), F32),
        vmem((3, 8, 128), F32),
        vmem((3, 8, 128), F32),
        vmem((8, 128), F32),
        dma((12,)),
        dma((4,)),
        dma((2,)),
        dma((14,)),
        dma((6,)),
        dma((6,)),
        dma((2,)),
        dma((5,)),
        dma((8,)),
        dma((5,)),
        dma((8,)),
        dma((4,)),
        dma((5,)),
        dma((1,)),
        pltpu.SemaphoreType.REGULAR((4,)),
    ]
    return pl.pallas_call(
        kernel,
        out_shape=jax.ShapeDtypeStruct(object_field.shape, F32),
        in_specs=[scalar, scalar] + [anywhere] * (3 + len(constants)),
        out_specs=inside,
        scratch_shapes=scratch,
        compiler_params=pltpu.CompilerParams(
            collective_id=0, has_side_effects=True, vmem_limit_bytes=60 << 20
        ),
        cost_estimate=pl.CostEstimate(
            flops=2_000_000_000, bytes_accessed=8_000_000, transcendentals=200_000
        ),
    )(row_offset, col_offset, object_field, probe, intensity, *constants)


def solution(mesh):
    placed = (
        P(None, ("outer", "inner"), None),
        P(None, ("outer", "inner"), None),
        P(("outer", "inner"), None),
        P(),
        P(),
    )
    return jax.shard_map(
        body,
        mesh=mesh,
        in_specs=placed,
        out_specs=P(None, ("outer", "inner"), None),
        check_vma=False,
    )
```

time: 92.2 us -> 69.8 us (0.76)
  local copies, waits for them, and re-layouts: 12.3 us -> 1.87 us
  Pallas kernels: 75.9 us -> 66.5 us
  other arithmetic: 2.09 us -> 0 us
    unnamed x24 -> x1, local copies, waits for them, and re-layouts: 12.3 us -> 1.87 us
    pallas_call x1, Pallas kernels: 75.9 us -> 66.5 us  [body(): pl.pallas_call(kernel, out_shape=jax.ShapeDtypeStruct(object_field.shape,...]
    div x1 -> x0, other arithmetic: 1.47 us -> none  [body(): return step / jnp.max(peak)]
where the time goes in v1:
time: 69.8 us; the launch traced here: 69.6 us
  Pallas kernels  66.5 us (95%)
  local copies, waits for them, and re-layouts  1.87 us (3%)
  between operations  1.3 us (2%)
    pallas_call x1, Pallas kernels, body(): pl.pallas_call(kernel, out_shape=jax.ShapeDtypeStruct(object_field.shape,...  66.5 us
    unnamed x1, local copies, waits for them, and re-layouts  1.87 us

profile of v1, /device:TPU:1, one launch (start us, length us, event | category | flops | bytes accessed | tf_op | source)
XLA Modules:
  0.0 69.6 jit_solution(18360627939657400328)
XLA Ops:
  1.3 66.5 %shard_map.136 = f32[2,8,8192]{2,1,0:T(8,128)} custom-call(s32[1]{0:T(128)S(6)} %copy.16.row_off, s32[1]{0:T(128)S(6)} %copy.17.col_off, f32[2,8,8192]{2,1,0:T(8,128)} %obj_hbm.1, f32[2,8,8192]{2,1,0:T(8,128)} %probe_hbm.1, f32[8,8192]{1,0:T(8,128)} %int_hbm.1, f32[2,1,8192]{2,1,0:T(1,128)} %constant.18.clone.col_chirp_hbm, ...), custom_call_target="tpu_custom_call" | custom-call | flops 2000000000 | bytes 8000000 | tf_op jit(solution)/shard_map/pallas_call | solution.py:775
  67.8 1.9 %copy.18 = f32[2,8,8192]{2,1,0:T(8,128)} copy(f32[2,8,8192]{2,1,0:T(8,128)} %shard_map.136) | data formatting | bytes 1048576

commit v2 on v1

--- a/solution.py
+++ b/solution.py
@@ -9,7 +9,6 @@
 from jax.sharding import PartitionSpec as P
 
 FLOOR_LEVEL = 0.1
-EARLY = 3
 MESH = pl.DeviceIdType.MESH
 CHIPS = 128
 F32 = jnp.float32
@@ -206,7 +205,7 @@
 
     loads = []
     pairs = (
-        (obj_hbm, obj),
+        (obj_hbm.at[0], obj.at[0]),
         (probe_hbm, probe),
         (int_hbm, inten.at[core]),
         (base_hbm.at[core], base),
@@ -218,11 +217,12 @@
         (last_back_hbm, last_back),
         (twiddle_hbm, twiddle),
         (first_back_hbm, first_back),
+        (obj_hbm.at[1], obj.at[1]),
     )
     for slot, (source, target) in enumerate(pairs):
-        copy = pltpu.make_async_copy(source, target, load_sem.at[slot])
-        copy.start()
-        loads.append(copy)
+        loads.append(pltpu.make_async_copy(source, target, load_sem.at[slot]))
+    for slot in (0, 2, 12):
+        loads[slot].start()
 
     barrier = pltpu.get_barrier_semaphore()
 
@@ -244,7 +244,6 @@
     tiles_by, lanes_by = cols_by // 128, cols_by % 128
     lane = lax.broadcasted_iota(jnp.int32, (8, 128), 1)
     sub = lax.broadcasted_iota(jnp.int32, (8, 128), 0)
-    loads[0].wait()
     for part in range(2):
         for row in (7,):
             arrived[pl.ds(part * 512 + row * 64, 64), :] = jnp.zeros((64, 128), F32)
@@ -266,6 +265,7 @@
             rolled[at, :] = jnp.where(wide_lane < lanes_by, pltpu.roll(moved, 1, 0), moved)
             return carry
 
+        loads[12 * part].wait()
         lax.fori_loop(0, 8, roll_step, 0)
         lax.fori_loop(0, 8, tile_step, 0)
         if part == 0:
@@ -281,18 +281,69 @@
         )
         shift.start()
         shifts.append(shift)
-    loads[2].wait()
-    share = pltpu.make_async_remote_copy(
-        src_ref=inten.at[core],
-        dst_ref=inten.at[core],
-        send_sem=int_sem.at[0],
-        recv_sem=int_sem.at[1],
-        device_id=sibling,
-        device_id_type=MESH,
-    )
-    share.start()
+        if part == 0:
+            loads[2].wait()
+            share = pltpu.make_async_remote_copy(
+                src_ref=inten.at[core],
+                dst_ref=inten.at[core],
+                send_sem=int_sem.at[0],
+                recv_sem=int_sem.at[1],
+                device_id=sibling,
+                device_id_type=MESH,
+            )
+            share.start()
+    for slot in (1, 3, 4, 5, 6, 7, 8, 9, 10, 11):
+        loads[slot].start()
     pl.semaphore_wait(gates.at[0], 6)
     tell(gates.at[1], [at_chip(2, 0, 0), at_chip(-2, 0, 0)])
+
+    pl.semaphore_wait(gates.at[1], 2)
+    tell(gates.at[2], [device_of(flip(chip, k << 5), core) for k in range(1, 4)])
+    share.wait_recv()
+    for c in range(2):
+
+        def spread_step(step, carry, c=c):
+            for inside in range(8):
+                at = step * 8 + inside
+                piece = inten[c, :, pl.ds(pl.multiple_of(at * 128, 128), 128)]
+                spread[pl.ds(c * 64 + at, 8, stride=128), :] = piece
+            return carry
+
+        lax.fori_loop(0, 8, spread_step, 0)
+    pl.semaphore_wait(gates.at[2], 3)
+    tell(gates.at[3], [device_of(flip(chip, k), core) for k in range(1, 4)])
+    for l in range(4):
+        shades_out[pl.ds(l, 128, stride=8), :] = jnp.transpose(spread[pl.ds(l * 128, 128), :])
+
+    for l in range(4, 8):
+        shades_out[pl.ds(l, 128, stride=8), :] = jnp.transpose(spread[pl.ds(l * 128, 128), :])
+    pl.semaphore_wait(gates.at[3], 3)
+
+    def send_shades(group):
+        def shade_step(step, carry):
+            target = flip(chip, group * 32 + step % 8 * 4 + step // 8 * 2 + core)
+            pltpu.make_async_remote_copy(
+                src_ref=tile(shades_out, target),
+                dst_ref=shades_in.at[chip // 2, chip % 2],
+                send_sem=shade_sem.at[0],
+                recv_sem=shade_sem.at[1 + group],
+                device_id=device_of(target, core),
+                device_id_type=MESH,
+            ).start()
+            return carry
+
+        lax.fori_loop((1 - core) if group == 0 else 0, 16, shade_step, 0)
+
+    for group in range(4):
+        send_shades(group)
+
+    @pl.when(core == 0)
+    def _():
+        own = pltpu.make_async_copy(
+            tile(shades_out, chip), shades_in.at[chip // 2, chip % 2], local_sem.at[0]
+        )
+        own.start()
+        own.wait()
 
     loads[1].wait()
 
@@ -305,8 +356,6 @@
 
     peak_own[0] = lax.fori_loop(0, 8, peak_step, jnp.zeros((8, 128), F32))
 
-    pl.semaphore_wait(gates.at[1], 2)
-    tell(gates.at[2], [device_of(flip(chip, k << 5), core) for k in range(1, 4)])
     loads[3].wait()
     loads[4].wait()
     chip_lane = lax.broadcasted_iota(jnp.int32, (64, 128), 1) == chip
@@ -322,57 +371,6 @@
             high_part, low_part = split(value)
             mixed[0, at, :] = high_part
             mixed[1, at, :] = low_part
-
-    pl.semaphore_wait(gates.at[2], 3)
-    tell(gates.at[3], [device_of(flip(chip, k), core) for k in range(1, 4)])
-    share.wait_recv()
-    for c in range(2):
-
-        def spread_step(step, carry, c=c):
-            for inside in range(8):
-                at = step * 8 + inside
-                piece = inten[c, :, pl.ds(pl.multiple_of(at * 128, 128), 128)]
-                spread[pl.ds(c * 64 + at, 8, stride=128), :] = piece
-            return carry
-
-        lax.fori_loop(0, 8, spread_step, 0)
-    for l in range(4):
-        shades_out[pl.ds(l, 128, stride=8), :] = jnp.transpose(spread[pl.ds(l * 128, 128), :])
-
-    for l in range(4, 8):
-        shades_out[pl.ds(l, 128, stride=8), :] = jnp.transpose(spread[pl.ds(l * 128, 128), :])
-    pl.semaphore_wait(gates.at[3], 3)
-
-    def send_shades(group):
-        def shade_step(step, carry):
-            target = flip(chip, group * 32 + step % 8 * 4 + step // 8 * 2 + core)
-            pltpu.make_async_remote_copy(
-                src_ref=tile(shades_out, target),
-                dst_ref=shades_in.at[chip // 2, chip % 2],
-                send_sem=shade_sem.at[0],
-                recv_sem=shade_sem.at[1 + group],
-                device_id=device_of(target, core),
-                device_id_type=MESH,
-            ).start()
-            return carry
-
-        lax.fori_loop(1 if group == 0 else 0, 16, shade_step, 0)
-        if group == 0:
-
-            @pl.when(core == 1)
-            def _():
-                shade_step(0, 0)
-
-            @pl.when(core == 0)
-            def _():
-                own = pltpu.make_async_copy(
-                    tile(shades_out, chip), shades_in.at[chip // 2, chip % 2], local_sem.at[0]
-                )
-                own.start()
-                own.wait()
-
-    for group in range(EARLY):
-        send_shades(group)
 
     for slot in (5, 6, 7):
         loads[slot].wait()
@@ -444,10 +442,11 @@
             return carry
 
         lax.fori_loop(1 if group == 0 else 0, 32, send_step, 0)
-        if group == 0:
-            own = pltpu.make_async_copy(tile(source, chip), tile(target, chip), local_sem.at[0])
-            own.start()
-            own.wait()
+
+    def keep_own(source, target):
+        own = pltpu.make_async_copy(tile(source, chip), tile(target, chip), local_sem.at[0])
+        own.start()
+        own.wait()
 
     def all_of(source, target, sem, rows, group=0):
         return pltpu.make_async_remote_copy(
@@ -461,11 +460,6 @@
 
     def got_group(source, target, sem, group):
         all_of(source, target, sem, 248 if group == 0 else 256, group).wait_recv()
-
-    for group in range(4):
-        send_group(field_out, field_in, field_sem, group)
-    for group in range(EARLY, 4):
-        send_shades(group)
 
     def peak_line(source, target, sem, count, by):
         copies = []
@@ -483,6 +477,9 @@
         return copies
 
     z_line = peak_line(peak_own.at[0], peak_z, z_sem, 8, 2)
+    for group in range(4):
+        send_group(field_out, field_in, field_sem, group)
+    keep_own(field_out, field_in)
 
 
     mine = (chip + core) % 2
@@ -524,10 +521,20 @@
                 shade = jnp.where(lane_group == want, pltpu.roll(part, by, 1), shade)
             factor[c, pl.ds(pl.multiple_of((y ^ group) * 64, 64), 64), :] = jnp.sqrt(shade)
 
-    passes = [pass_shades(group) for group in range(EARLY)]
-    for group in range(EARLY):
-        passes[group].wait()
-        make_factor(group)
+    for copy in z_line:
+        copy.wait_recv()
+    best = peak_own[0]
+    for k in range(7):
+        best = jnp.maximum(best, peak_z[k])
+    peak_own[1] = best
+    y_line = peak_line(peak_own.at[1], peak_y, y_sem, 4, 5)
+    passes = [pass_shades(group) for group in range(4)]
+    for copy in y_line:
+        copy.wait_recv()
+    for k in range(3):
+        best = jnp.maximum(best, peak_y[k])
+    peak_own[2] = best
+    x_line = peak_line(peak_own.at[2], peak_x, x_sem, 4, 0)
 
     sent_half = (mixed.at[0, :, pl.ds(256, 256)], mixed.at[1, :, pl.ds(256, 256)])
     kept_half = (mixed.at[0, :, pl.ds(0, 256)], mixed.at[1, :, pl.ds(0, 256)])
@@ -573,21 +580,30 @@
         mix_kept[rows, :] = three(dot, joined, (kept_half[0][...], kept_half[1][...]))
         if group > 0:
             prepare(group - 1)
-    for copy in z_line:
-        copy.wait_recv()
-    best = peak_own[0]
-    for k in range(7):
-        best = jnp.maximum(best, peak_z[k])
-    peak_own[1] = best
-    y_line = peak_line(peak_own.at[1], peak_y, y_sem, 4, 5)
-    late = [pass_shades(group) for group in range(EARLY, 4)]
+        else:
+            for early in range(4):
+                passes[early].wait()
+                make_factor(early)
+        if group == 1:
+            for copy in x_line:
+                copy.wait_recv()
+            for k in range(3):
+                best = jnp.maximum(best, peak_x[k])
+            peak_own[3] = best
+            c_line = pltpu.make_async_remote_copy(
+                src_ref=peak_own.at[3],
+                dst_ref=peak_c,
+                send_sem=c_sem.at[0],
+                recv_sem=c_sem.at[1],
+                device_id=sibling,
+                device_id_type=MESH,
+            )
+            c_line.start()
     prepare(3)
-    for group in range(EARLY, 4):
-        late[group - EARLY].wait()
-        make_factor(group)
-    for block in range(4):
-        value = three(dot, (last[0, block], last[1, block]), (data[0], data[1]))
-        rows = pl.ds(block * 64, 64)
+    for group in range(4):
+        here = y ^ group
+        value = three(dot, (last[0, here], last[1, here]), (data[0], data[1]))
+        rows = pl.ds(pl.multiple_of(here * 64, 64), 64)
         for k2 in range(2):
             lanes = pl.ds(k2 * 128, 128)
             real = value[:64, k2 * 128 : (k2 + 1) * 128]
@@ -595,72 +611,61 @@
             size = jnp.sqrt(real * real + imag * imag)
             scale = factor[k2, rows, :] / jnp.maximum(size, FLOOR_LEVEL)
             for ri, part in enumerate((real * scale, imag * scale)):
+                at = pl.ds(pl.multiple_of(ri * 256 + here * 64, 64), 64)
                 high_part, low_part = split(part)
-                again[0, pl.ds(ri * 256 + block * 64, 64), lanes] = high_part
-                again[1, pl.ds(ri * 256 + block * 64, 64), lanes] = low_part
+                again[0, at, lanes] = high_part
+                again[1, at, lanes] = low_part
     loads[9].wait()
     own_core = core == 0
     swaps = []
-    for half in range(2):
-        for group in (2 * half, 2 * half + 1):
-            here = y ^ group
-            rows = pl.ds(pl.multiple_of(here * 64, 64), 64)
-            value = three(dot, (last_back[0, here], last_back[1, here]), (again[0], again[1]))
-            parts = []
-            for k2 in range(2):
-                real = value[:64, k2 * 128 : (k2 + 1) * 128]
-                imag = value[64:, k2 * 128 : (k2 + 1) * 128]
-                turn_r, turn_i = twiddle[k2, 0, rows, :], twiddle[k2, 1, rows, :]
-                parts.append(
-                    jnp.concatenate(
-                        [real * turn_r + imag * turn_i, imag * turn_r - real * turn_i], axis=1
-                    )
+
+    def inverse_group(group):
+        here = y ^ group
+        rows = pl.ds(pl.multiple_of(here * 64, 64), 64)
+        value = three(dot, (last_back[0, here], last_back[1, here]), (again[0], again[1]))
+        parts = []
+        for k2 in range(2):
+            real = value[:64, k2 * 128 : (k2 + 1) * 128]
+            imag = value[64:, k2 * 128 : (k2 + 1) * 128]
+            turn_r, turn_i = twiddle[k2, 0, rows, :], twiddle[k2, 1, rows, :]
+            parts.append(
+                jnp.concatenate(
+                    [real * turn_r + imag * turn_i, imag * turn_r - real * turn_i], axis=1
                 )
-            plus, minus = parts[0] + parts[1], parts[0] - parts[1]
-            part_out[rows, :] = jnp.where(own_core, minus, plus)
-            part_own[rows, :] = jnp.where(own_core, plus, minus)
-        rows = pl.ds(pl.multiple_of((y // 2 ^ half) * 128, 128), 128)
+            )
+        plus, minus = parts[0] + parts[1], parts[0] - parts[1]
+        part_out[rows, :] = jnp.where(own_core, minus, plus)
+        part_own[rows, :] = jnp.where(own_core, plus, minus)
         swap = pltpu.make_async_remote_copy(
             src_ref=part_out.at[rows],
             dst_ref=part_in.at[rows],
-            send_sem=part_sem.at[half],
-            recv_sem=part_sem.at[2 + half],
+            send_sem=part_sem.at[group],
+            recv_sem=part_sem.at[4 + group],
             device_id=sibling,
             device_id_type=MESH,
         )
         swap.start()
         swaps.append(swap)
-    for copy in y_line:
-        copy.wait_recv()
-    for k in range(3):
-        best = jnp.maximum(best, peak_y[k])
-    peak_own[2] = best
-    x_line = peak_line(peak_own.at[2], peak_x, x_sem, 4, 0)
-    for half in range(2):
-        swaps[half].wait_recv()
-        rows = pl.ds(pl.multiple_of((y // 2 ^ half) * 128, 128), 128)
+
+    def back_group(group):
+        swaps[group].wait_recv()
+        here = y ^ group
+        rows = pl.ds(pl.multiple_of(here * 64, 64), 64)
         joined = split(jnp.concatenate([part_own[rows, :], part_in[rows, :]], axis=1))
         result = three(dot_t, joined, (mixed[0], mixed[1]))
-        for low in range(2):
-            for digit in range(4):
-                at = pl.multiple_of((y // 2 ^ half) * 512 + low * 256 + digit * 64, 64)
-                back_out[pl.ds(at, 64), :] = result[low * 64 : (low + 1) * 64, digit * 128 : (digit + 1) * 128]
-        for group in (2 * half, 2 * half + 1):
-            send_group(back_out, back_in, back_sem, group)
-    for copy in x_line:
-        copy.wait_recv()
-    for k in range(3):
-        best = jnp.maximum(best, peak_x[k])
-    peak_own[3] = best
-    c_line = pltpu.make_async_remote_copy(
-        src_ref=peak_own.at[3],
-        dst_ref=peak_c,
-        send_sem=c_sem.at[0],
-        recv_sem=c_sem.at[1],
-        device_id=sibling,
-        device_id_type=MESH,
-    )
-    c_line.start()
+        for digit in range(4):
+            at = pl.ds(pl.multiple_of(here * 256 + digit * 64, 64), 64)
+            back_out[at, :] = result[:, digit * 128 : (digit + 1) * 128]
+        send_group(back_out, back_in, back_sem, group)
+        if group == 0:
+            keep_own(back_out, back_in)
+
+    for group in range(3):
+        inverse_group(group)
+    back_group(0)
+    inverse_group(3)
+    for group in range(1, 4):
+        back_group(group)
     c_line.wait_recv()
     gain = 1.0 / jnp.max(jnp.maximum(best, peak_c[...]))
 
@@ -756,7 +761,7 @@
         vmem((3, 8, 128), F32),
         vmem((3, 8, 128), F32),
         vmem((8, 128), F32),
-        dma((12,)),
+        dma((13,)),
         dma((4,)),
         dma((2,)),
         dma((14,)),
@@ -767,14 +772,14 @@
         dma((8,)),
         dma((5,)),
         dma((8,)),
-        dma((4,)),
+        dma((8,)),
         dma((5,)),
         dma((1,)),
         pltpu.SemaphoreType.REGULAR((4,)),
     ]
     return pl.pallas_call(
         kernel,
-        out_shape=jax.ShapeDtypeStruct(object_field.shape, F32),
+        out_shape=pltpu.VMEM(object_field.shape, F32),
         in_specs=[scalar, scalar] + [anywhere] * (3 + len(constants)),
         out_specs=inside,
         scratch_shapes=scratch,

time: 69.8 us -> 67.8 us (0.971)
  local copies, waits for them, and re-layouts: 1.87 us -> 0.8 us
  Pallas kernels: 66.5 us -> 65.6 us
    unnamed x1, local copies, waits for them, and re-layouts: 1.87 us -> 0.8 us
    pallas_call x1, Pallas kernels: 66.5 us -> 65.6 us  [body(): pl.pallas_call(kernel, out_shape=pltpu.VMEM(object_field.shape, F32), in_...]
where the time goes in v2:
time: 67.8 us; the launch traced here: 67.7 us
  Pallas kernels  65.6 us (97%)
  between operations  1.3 us (2%)
  local copies, waits for them, and re-layouts  0.8 us (1%)
    pallas_call x1, Pallas kernels, body(): pl.pallas_call(kernel, out_shape=pltpu.VMEM(object_field.shape, F32), in_...  65.6 us

profile of v2, /device:TPU:1, one launch (start us, length us, event | category | flops | bytes accessed | tf_op | source)
XLA Modules:
  0.0 67.7 jit_solution(1636644839864239737)
XLA Ops:
  1.3 65.6 %shard_map.136 = f32[2,8,8192]{2,1,0:T(8,128)S(1)} custom-call(s32[1]{0:T(128)S(6)} %copy.17.row_off, s32[1]{0:T(128)S(6)} %copy.18.col_off, f32[2,8,8192]{2,1,0:T(8,128)} %obj_hbm.1, f32[2,8,8192]{2,1,0:T(8,128)} %probe_hbm.1, f32[8,8192]{1,0:T(8,128)} %int_hbm.1, f32[2,1,8192]{2,1,0:T(1,128)} %constant.18.clone.col_chirp_hbm, ...), custom_call_target="tpu_custom_call" | custom-call | flops 2000000000 | bytes 8000000 | tf_op jit(solution)/shard_map/pallas_call | solution.py:780
  66.9 0.8 %copy.16 = f32[2,8,8192]{2,1,0:T(8,128)} copy(f32[2,8,8192]{2,1,0:T(8,128)S(1)} %shard_map.136) | data formatting | bytes 1048576

commit v3 on v2

--- a/solution.py
+++ b/solution.py
@@ -9,6 +9,7 @@
 from jax.sharding import PartitionSpec as P
 
 FLOOR_LEVEL = 0.1
+ORDER = (2, 3, 1, 0)
 MESH = pl.DeviceIdType.MESH
 CHIPS = 128
 F32 = jnp.float32
@@ -114,6 +115,15 @@
     return (z // 2) * 2 + core, (chip // 32) * 8 + (chip % 4) * 2 + z % 2
 
 
+def far_first(step):
+    swapped = step ^ 2
+    return swapped ^ (1 - swapped // 2)
+
+
+def far_first_of_eight(step):
+    return jnp.where(step < 4, step + 4, far_first(step % 4))
+
+
 def flip(chip, offset):
     return chip ^ offset
 
@@ -153,6 +163,7 @@
     rolled,
     arrived,
     wave,
+    lifted,
     turned,
     field_out,
     field_in,
@@ -321,7 +332,8 @@
 
     def send_shades(group):
         def shade_step(step, carry):
-            target = flip(chip, group * 32 + step % 8 * 4 + step // 8 * 2 + core)
+            offset = far_first_of_eight(step % 8) * 4 + (1 - step // 8) * 2 + core
+            target = flip(chip, group * 32 + offset)
             pltpu.make_async_remote_copy(
                 src_ref=tile(shades_out, target),
                 dst_ref=shades_in.at[chip // 2, chip % 2],
@@ -332,9 +344,9 @@
             ).start()
             return carry
 
-        lax.fori_loop((1 - core) if group == 0 else 0, 16, shade_step, 0)
-
-    for group in range(4):
+        lax.fori_loop(0, 15 + core if group == 0 else 16, shade_step, 0)
+
+    for group in ORDER:
         send_shades(group)
 
     @pl.when(core == 0)
@@ -382,31 +394,38 @@
         col_re, col_im = col_chirp[0, :, at], col_chirp[1, :, at]
         return row_re * col_re - row_im * col_im, row_re * col_im + row_im * col_re
 
-    for shift in shifts:
-        shift.wait_recv()
-
-    def wave_step(step, carry):
+    def lift_step(step, carry):
         for inside in range(8):
             index = step * 8 + inside
             at = pl.ds(pl.multiple_of(index * 128, 128), 128)
-            views = []
-            for part in range(2):
-                rows = pl.ds(part * 512 + index, 8, stride=64)
-                views.append(jnp.where(sub < rows_by, arrived[rows, :], rolled[rows, :]))
             probe_re, probe_im = probe[0, :, at], probe[1, :, at]
-            real = probe_re * views[0] - probe_im * views[1]
-            imag = probe_re * views[1] + probe_im * views[0]
-            wave[0, :, at] = real
-            wave[1, :, at] = imag
             chirp_re, chirp_im = chirp_at(at)
-            real, imag = real * chirp_re - imag * chirp_im, real * chirp_im + imag * chirp_re
-            even = jnp.where(lane < 64, real, pltpu.roll(imag, 64, 1))
-            odd = jnp.where(lane < 64, pltpu.roll(real, 64, 1), imag)
-            turned[pl.ds(index, 8, stride=128), :] = even
-            turned[pl.ds(64 + index, 8, stride=128), :] = odd
+            lifted[pl.ds(index, 8, stride=64), :] = probe_re * chirp_re - probe_im * chirp_im
+            lifted[pl.ds(512 + index, 8, stride=64), :] = probe_re * chirp_im + probe_im * chirp_re
         return carry
 
-    lax.fori_loop(0, 8, wave_step, 0)
+    lax.fori_loop(0, 8, lift_step, 0)
+
+    for shift in shifts:
+        shift.wait_recv()
+    left = wide_lane < 64
+
+    def wave_row(row, carry):
+        re_at = pl.ds(pl.multiple_of(row * 64, 64), 64)
+        im_at = pl.ds(pl.multiple_of(512 + row * 64, 64), 64)
+        from_before = jnp.full((64, 128), row, jnp.int32) < rows_by
+        view_re = jnp.where(from_before, arrived[re_at, :], rolled[re_at, :])
+        view_im = jnp.where(from_before, arrived[im_at, :], rolled[im_at, :])
+        lift_re, lift_im = lifted[re_at, :], lifted[im_at, :]
+        real = lift_re * view_re - lift_im * view_im
+        imag = lift_re * view_im + lift_im * view_re
+        even = jnp.where(left, real, pltpu.roll(imag, 64, 1))
+        odd = jnp.where(left, pltpu.roll(real, 64, 1), imag)
+        turned[pl.ds(pl.multiple_of(row * 128, 128), 64), :] = even
+        turned[pl.ds(pl.multiple_of(row * 128 + 64, 64), 64), :] = odd
+        return carry
+
+    lax.fori_loop(0, 8, wave_row, 0)
 
     def times_i(value):
         half = lax.broadcasted_iota(jnp.int32, value.shape, 1) < 64
@@ -430,7 +449,8 @@
 
     def send_group(source, target, sem, group):
         def send_step(step, carry):
-            to = flip(chip, group * 32 + step % 8 * 4 + step // 8)
+            offset = group * 32 + far_first_of_eight(step % 8) * 4 + far_first(step // 8)
+            to = flip(chip, offset)
             pltpu.make_async_remote_copy(
                 src_ref=tile(source, to),
                 dst_ref=tile(target, chip),
@@ -441,7 +461,7 @@
             ).start()
             return carry
 
-        lax.fori_loop(1 if group == 0 else 0, 32, send_step, 0)
+        lax.fori_loop(0, 31 if group == 0 else 32, send_step, 0)
 
     def keep_own(source, target):
         own = pltpu.make_async_copy(tile(source, chip), tile(target, chip), local_sem.at[0])
@@ -477,7 +497,7 @@
         return copies
 
     z_line = peak_line(peak_own.at[0], peak_z, z_sem, 8, 2)
-    for group in range(4):
+    for group in ORDER:
         send_group(field_out, field_in, field_sem, group)
     keep_own(field_out, field_in)
 
@@ -536,6 +556,21 @@
     peak_own[2] = best
     x_line = peak_line(peak_own.at[2], peak_x, x_sem, 4, 0)
 
+    def wave_step(step, carry):
+        for inside in range(8):
+            index = step * 8 + inside
+            at = pl.ds(pl.multiple_of(index * 128, 128), 128)
+            views = []
+            for part in range(2):
+                rows = pl.ds(part * 512 + index, 8, stride=64)
+                views.append(jnp.where(sub < rows_by, arrived[rows, :], rolled[rows, :]))
+            probe_re, probe_im = probe[0, :, at], probe[1, :, at]
+            wave[0, :, at] = probe_re * views[0] - probe_im * views[1]
+            wave[1, :, at] = probe_re * views[1] + probe_im * views[0]
+        return carry
+
+    lax.fori_loop(0, 8, wave_step, 0)
+
     sent_half = (mixed.at[0, :, pl.ds(256, 256)], mixed.at[1, :, pl.ds(256, 256)])
     kept_half = (mixed.at[0, :, pl.ds(0, 256)], mixed.at[1, :, pl.ds(0, 256)])
     mixes = []
@@ -543,9 +578,9 @@
     loads[8].wait()
     loads[10].wait()
 
-    def prepare(group):
-        mixes[group].wait_recv()
-        here = y ^ group
+    def prepare(turn_at):
+        mixes[turn_at].wait_recv()
+        here = y ^ ORDER[turn_at]
         rows = pl.ds(pl.multiple_of(here * 64, 64), 64)
         kept, got = mix_kept[rows, :], mix_in[rows, :]
         for k2, total in enumerate((kept + got, (kept - got) * sign)):
@@ -560,7 +595,7 @@
                 data[0, at, lanes] = high_part
                 data[1, at, lanes] = low_part
 
-    for group in range(4):
+    for turn_at, group in enumerate(ORDER):
         got_group(field_out, field_in, field_sem, group)
         here = y ^ group
         pieces = [field_in[pl.ds(pl.multiple_of(here * 256 + digit * 64, 64), 64), :] for digit in range(4)]
@@ -570,21 +605,21 @@
         mix = pltpu.make_async_remote_copy(
             src_ref=mix_out.at[rows],
             dst_ref=mix_in.at[rows],
-            send_sem=mix_sem.at[group],
-            recv_sem=mix_sem.at[4 + group],
+            send_sem=mix_sem.at[turn_at],
+            recv_sem=mix_sem.at[4 + turn_at],
             device_id=sibling,
             device_id_type=MESH,
         )
         mix.start()
         mixes.append(mix)
         mix_kept[rows, :] = three(dot, joined, (kept_half[0][...], kept_half[1][...]))
-        if group > 0:
-            prepare(group - 1)
+        if turn_at > 0:
+            prepare(turn_at - 1)
         else:
             for early in range(4):
                 passes[early].wait()
                 make_factor(early)
-        if group == 1:
+        if turn_at == 1:
             for copy in x_line:
                 copy.wait_recv()
             for k in range(3):
@@ -648,7 +683,7 @@
         swaps.append(swap)
 
     def back_group(group):
-        swaps[group].wait_recv()
+        swaps[ORDER.index(group)].wait_recv()
         here = y ^ group
         rows = pl.ds(pl.multiple_of(here * 64, 64), 64)
         joined = split(jnp.concatenate([part_own[rows, :], part_in[rows, :]], axis=1))
@@ -660,11 +695,11 @@
         if group == 0:
             keep_own(back_out, back_in)
 
-    for group in range(3):
+    for group in ORDER[:3]:
         inverse_group(group)
-    back_group(0)
-    inverse_group(3)
-    for group in range(1, 4):
+    back_group(ORDER[0])
+    inverse_group(ORDER[3])
+    for group in ORDER[1:]:
         back_group(group)
     c_line.wait_recv()
     gain = 1.0 / jnp.max(jnp.maximum(best, peak_c[...]))
@@ -738,6 +773,7 @@
         state,
         state,
         vmem((2, 8, 8192), F32),
+        state,
         state,
         state,
         state,

time: 67.8 us -> 64.4 us (0.950)
  Pallas kernels: 65.6 us -> 62.2 us
    pallas_call x1, Pallas kernels: 65.6 us -> 62.2 us  [body(): pl.pallas_call(kernel, out_shape=pltpu.VMEM(object_field.shape, F32), in_...]
where the time goes in v3:
time: 64.4 us; the launch traced here: 64.3 us
  Pallas kernels  62.2 us (97%)
  between operations  1.3 us (2%)
  local copies, waits for them, and re-layouts  0.8 us (1%)
    pallas_call x1, Pallas kernels, body(): pl.pallas_call(kernel, out_shape=pltpu.VMEM(object_field.shape, F32), in_...  62.2 us

profile of v3, /device:TPU:1, one launch (start us, length us, event | category | flops | bytes accessed | tf_op | source)
XLA Modules:
  0.0 64.3 jit_solution(6967026435798244379)
XLA Ops:
  1.3 62.2 %shard_map.136 = f32[2,8,8192]{2,1,0:T(8,128)S(1)} custom-call(s32[1]{0:T(128)S(6)} %copy.17.row_off, s32[1]{0:T(128)S(6)} %copy.18.col_off, f32[2,8,8192]{2,1,0:T(8,128)} %obj_hbm.1, f32[2,8,8192]{2,1,0:T(8,128)} %probe_hbm.1, f32[8,8192]{1,0:T(8,128)} %int_hbm.1, f32[2,1,8192]{2,1,0:T(1,128)} %constant.18.clone.col_chirp_hbm, ...), custom_call_target="tpu_custom_call" | custom-call | flops 2000000000 | bytes 8000000 | tf_op jit(solution)/shard_map/pallas_call | solution.py:816
  63.5 0.8 %copy.16 = f32[2,8,8192]{2,1,0:T(8,128)} copy(f32[2,8,8192]{2,1,0:T(8,128)S(1)} %shard_map.136) | data formatting | bytes 1048576

commit v4 on v3

--- a/solution.py
+++ b/solution.py
@@ -182,6 +182,7 @@
     part_out,
     part_in,
     part_own,
+    landed,
     peak_own,
     peak_z,
     peak_y,
@@ -705,13 +706,21 @@
     gain = 1.0 / jnp.max(jnp.maximum(best, peak_c[...]))
 
     loads[11].wait()
-    for group in range(4):
+    for group in ORDER:
         got_group(back_out, back_in, back_sem, group)
-
-    def store_turned(row, value):
-        turned[pl.ds(row * 128, 128), :] = value
-
-    first_step(lambda row: back_in[pl.ds(row, 128, stride=8), :], first_back, store_turned)
+        here = y ^ group
+        for row in range(8):
+            value = back_in[pl.ds(here * 256 + row, 32, stride=8), :]
+            lanes = pl.ds(row % 2 * 128, 128)
+            for base_at, part in ((0, value), (128, times_i(value))):
+                at = pl.ds(pl.multiple_of(base_at + here * 32, 32), 32)
+                high_part, low_part = split(part)
+                landed[0, row // 2, at, lanes] = high_part
+                landed[1, row // 2, at, lanes] = low_part
+    for pair in range(4):
+        result = three(dot, (first_back[0], first_back[1]), (landed[0, pair], landed[1, pair]))
+        turned[pl.ds(2 * pair * 128, 128), :] = result[:, :128]
+        turned[pl.ds((2 * pair + 1) * 128, 128), :] = result[:, 128:]
 
     def last_step(step, carry):
         for inside in range(8):
@@ -792,6 +801,7 @@
         vmem((256, 256), F32),
         vmem((256, 256), F32),
         vmem((256, 256), F32),
+        vmem((2, 4, 256, 256), BF16),
         vmem((4, 8, 128), F32),
         vmem((7, 8, 128), F32),
         vmem((3, 8, 128), F32),

time: 64.4 us -> 64.4 us (level)
  no operation moved by 1% of the time
where the time goes in v4:
time: 64.4 us; the launch traced here: 64.3 us
  Pallas kernels  62.2 us (97%)
  between operations  1.3 us (2%)
  local copies, waits for them, and re-layouts  0.8 us (1%)
    pallas_call x1, Pallas kernels, body(): pl.pallas_call(kernel, out_shape=pltpu.VMEM(object_field.shape, F32), in_...  62.2 us

profile of v4, /device:TPU:1, one launch (start us, length us, event | category | flops | bytes accessed | tf_op | source)
XLA Modules:
  0.0 64.3 jit_solution(506702363990431274)
XLA Ops:
  1.3 62.2 %shard_map.136 = f32[2,8,8192]{2,1,0:T(8,128)S(1)} custom-call(s32[1]{0:T(128)S(6)} %copy.17.row_off, s32[1]{0:T(128)S(6)} %copy.18.col_off, f32[2,8,8192]{2,1,0:T(8,128)} %obj_hbm.1, f32[2,8,8192]{2,1,0:T(8,128)} %probe_hbm.1, f32[8,8192]{1,0:T(8,128)} %int_hbm.1, f32[2,1,8192]{2,1,0:T(1,128)} %constant.18.clone.col_chirp_hbm, ...), custom_call_target="tpu_custom_call" | custom-call | flops 2000000000 | bytes 8000000 | tf_op jit(solution)/shard_map/pallas_call | solution.py:826
  63.5 0.8 %copy.16 = f32[2,8,8192]{2,1,0:T(8,128)} copy(f32[2,8,8192]{2,1,0:T(8,128)S(1)} %shard_map.136) | data formatting | bytes 1048576

commit v5 on v4

--- a/solution.py
+++ b/solution.py
@@ -72,6 +72,8 @@
     for name, sign in (("last", 1.0), ("last_back", -1.0)):
         whole = np.block([[last.real, -sign * last.imag], [sign * last.imag, last.real]])
         blocks = whole.reshape(2, 4, 64, 512).transpose(1, 0, 2, 3).reshape(4, 128, 512)
+        if name == "last":
+            blocks = blocks.reshape(4, 128, 2, 4, 64).transpose(0, 3, 1, 2, 4).reshape(4, 4, 128, 128)
         tables[name] = split_table(blocks)
     klow = np.arange(128) // 32
     twiddle = np.stack([turn(n[:, None] * (klow[None, :] + 4 * k2), 2048) for k2 in range(2)]) / 4096.0
@@ -172,6 +174,7 @@
     mix_in,
     mix_kept,
     data,
+    partial,
     again,
     factor,
     spread,
@@ -591,10 +594,10 @@
             for ri, value in enumerate(
                 (real * turn_r - imag * turn_i, real * turn_i + imag * turn_r)
             ):
-                at = pl.ds(pl.multiple_of(ri * 256 + here * 64, 64), 64)
+                at = pl.ds(ri * 64, 64)
                 high_part, low_part = split(value)
-                data[0, at, lanes] = high_part
-                data[1, at, lanes] = low_part
+                data[0, here, at, lanes] = high_part
+                data[1, here, at, lanes] = low_part
 
     for turn_at, group in enumerate(ORDER):
         got_group(field_out, field_in, field_sem, group)
@@ -635,10 +638,18 @@
                 device_id_type=MESH,
             )
             c_line.start()
+    ready = [y ^ group for group in ORDER[:3]]
+    final = y ^ ORDER[3]
+    given = [jnp.concatenate([data[at, q] for q in ready], axis=0) for at in range(2)]
+    for here in range(4):
+        table = [jnp.concatenate([last[at, here, q] for q in ready], axis=1) for at in range(2)]
+        partial[here] = three(dot, table, given)
     prepare(3)
     for group in range(4):
         here = y ^ group
-        value = three(dot, (last[0, here], last[1, here]), (data[0], data[1]))
+        value = partial[here] + three(
+            dot, (last[0, here, final], last[1, here, final]), (data[0, final], data[1, final])
+        )
         rows = pl.ds(pl.multiple_of(here * 64, 64), 64)
         for k2 in range(2):
             lanes = pl.ds(k2 * 128, 128)
@@ -776,7 +787,7 @@
         vmem((2, 128, 256), BF16),
         vmem((2, 64, 128), F32),
         vmem((512, 512), F32),
-        vmem((2, 4, 128, 512), BF16),
+        vmem((2, 4, 4, 128, 128), BF16),
         vmem((2, 4, 128, 512), BF16),
         vmem((2, 2, 256, 128), F32),
         state,
@@ -790,7 +801,8 @@
         vmem((256, 256), F32),
         vmem((256, 256), F32),
         vmem((256, 256), F32),
-        vmem((2, 512, 256), BF16),
+        vmem((2, 4, 128, 256), BF16),
+        vmem((4, 128, 256), F32),
         vmem((2, 512, 256), BF16),
         vmem((2, 256, 128), F32),
         state,

time: 64.4 us -> 64.6 us (level)
  no operation moved by 1% of the time
where the time goes in v5:
time: 64.6 us; the launch traced here: 64.5 us
  Pallas kernels  62.4 us (97%)
  between operations  1.3 us (2%)
  local copies, waits for them, and re-layouts  0.8 us (1%)
    pallas_call x1, Pallas kernels, body(): pl.pallas_call(kernel, out_shape=pltpu.VMEM(object_field.shape, F32), in_...  62.4 us

profile of v5, /device:TPU:1, one launch (start us, length us, event | category | flops | bytes accessed | tf_op | source)
XLA Modules:
  0.0 64.5 jit_solution(494149492482837850)
XLA Ops:
  1.3 62.4 %shard_map.136 = f32[2,8,8192]{2,1,0:T(8,128)S(1)} custom-call(s32[1]{0:T(128)S(6)} %copy.17.row_off, s32[1]{0:T(128)S(6)} %copy.18.col_off, f32[2,8,8192]{2,1,0:T(8,128)} %obj_hbm.1, f32[2,8,8192]{2,1,0:T(8,128)} %probe_hbm.1, f32[8,8192]{1,0:T(8,128)} %int_hbm.1, f32[2,1,8192]{2,1,0:T(1,128)} %constant.18.clone.col_chirp_hbm, ...), custom_call_target="tpu_custom_call" | custom-call | flops 2000000000 | bytes 8000000 | tf_op jit(solution)/shard_map/pallas_call | solution.py:838
  63.7 0.8 %copy.16 = f32[2,8,8192]{2,1,0:T(8,128)} copy(f32[2,8,8192]{2,1,0:T(8,128)S(1)} %shard_map.136) | data formatting | bytes 1048576
